TPU v7x, 512 devices: a whole 4x4x16 slice. The times are simulated.
512 devices in a mesh: row: 32 (over x, z_lo), ch: 16 (over y, z_hi, core).
Axes of the slice: x: 4, y: 4, z: 16 (z_hi: 2, z_lo: 8; z = z_hi * 8 + z_lo), core: 2. Of those that a mesh axis runs over, the one named last changes fastest.
Arguments:
- pair: float32 [256, 256, 128], P('row', 'ch'), may hold values from -6 to 6
- pair_mask: int32 [256, 256], P('row', 'ch'), may hold values 0 or 1
- w_in: float32 [128, 512], replicated, may hold values from -0.5 to 0.5
- w_gate: float32 [128, 128], replicated, may hold values from -0.5 to 0.5
- w_out: float32 [128, 128], replicated, may hold values from -0.5 to 0.5
- cotangent: float32 [256, 256, 128], P('row', 'ch'), may hold values from -6 to 6
Outputs:
- update: float32 [256, 256, 128], P('row', 'ch')
- d_pair: float32 [256, 256, 128], P('row', 'ch')
- d_w_in: float32 [128, 512], replicated
- d_w_gate: float32 [128, 128], replicated
- d_w_out: float32 [128, 128], replicated
All inputs are finite; a program needn't handle non-finite values. No bound on the sum of `pair_mask` on one device may be relied on, other than what follows from the above.
Results may differ from a plain program's by a relative error of at most 0.00014.
Values sent between devices are 32-bit elements; how exact they have to be, the bound alone decides.
No kernel may reach another device: no remote copies, remote signals or barrier semaphores. Data moves between devices by JAX's collectives and lax.ppermute only.
A program may use at most 64 MiB of HBM per device.

v0:
```python
import jax
import jax.numpy as jnp
from jax import lax
from jax.sharding import PartitionSpec as P


def norm_along(values, axis):
    center = values - jnp.mean(values, axis=axis, keepdims=True)
    spread = jnp.mean(center * center, axis=axis, keepdims=True)
    return center / jnp.sqrt(spread + 1e-05)


def project(pair, pair_mask, w_in, w_gate):
    highest = lax.Precision.HIGHEST
    normed_pair = norm_along(pair, 2)
    projected = jnp.einsum("ikc,cf->fik", normed_pair, w_in, precision=highest)
    hidden = projected.shape[0] // 4
    maskf = pair_mask.astype(jnp.float32)
    left = maskf * jax.nn.sigmoid(projected[:hidden]) * projected[hidden : 2 * hidden]
    right = maskf * jax.nn.sigmoid(projected[2 * hidden : 3 * hidden]) * projected[3 * hidden :]
    gate = jax.nn.sigmoid(jnp.einsum("ikc,cd->ikd", normed_pair, w_gate, precision=highest))
    return (left, right, gate)


def finish(triangle, w_out):
    normed_tri = norm_along(triangle, 0)
    return jnp.einsum("hij,hc->ijc", normed_tri, w_out, precision=lax.Precision.HIGHEST)


def shards(pair, pair_mask, w_in, w_gate, w_out, cotangent):
    highest = lax.Precision.HIGHEST
    local_rows = pair.shape[0]

    def apply_in(pair_in, win_in, wgate_in):
        return project(pair_in, pair_mask, win_in, wgate_in)

    (left, right, gate), pull_in = jax.vjp(apply_in, pair, w_in, w_gate)
    left_c, right_c = (
        lax.all_to_all(left, "ch", split_axis=0, concat_axis=2, tiled=True),
        lax.all_to_all(right, "ch", split_axis=0, concat_axis=2, tiled=True),
    )
    right_all = lax.all_gather(right_c, "row", axis=1, tiled=True)
    tri_c = jnp.einsum("hik,hjk->hij", left_c, right_all, precision=highest)
    triangle = lax.all_to_all(tri_c, "ch", split_axis=2, concat_axis=0, tiled=True)
    out_proj, pull_out = jax.vjp(finish, triangle, w_out)
    update = gate * out_proj
    d_tri, d_wout = pull_out(cotangent * gate)
    d_gate = cotangent * out_proj
    d_tri_c = lax.all_to_all(d_tri, "ch", split_axis=0, concat_axis=2, tiled=True)
    d_left_c = jnp.einsum("hij,hjk->hik", d_tri_c, right_all, precision=highest)
    d_right_t = lax.psum_scatter(
        jnp.einsum("hij,hik->jhk", d_tri_c, left_c, precision=highest),
        "row",
        scatter_dimension=0,
        tiled=True,
    )
    d_right_c = jnp.transpose(d_right_t, (1, 0, 2))
    d_left, d_right = (
        lax.all_to_all(d_left_c, "ch", split_axis=2, concat_axis=0, tiled=True),
        lax.all_to_all(d_right_c, "ch", split_axis=2, concat_axis=0, tiled=True),
    )
    d_pair, d_win, d_wgate = pull_in((d_left, d_right, d_gate))
    sum_win, sum_wgate, sum_wout = lax.psum((d_win, d_wgate, d_wout), ("row", "ch"))
    scale = 1.0 / (local_rows * lax.axis_size("row"))
    return (update, d_pair, sum_win * scale, sum_wgate * scale, sum_wout * scale)


def solution(mesh):
    in_specs = (P("row", "ch", None), P("row", "ch"), P(), P(), P(), P("row", "ch", None))
    out_specs = (P("row", "ch", None), P("row", "ch", None), P(), P(), P())
    return jax.shard_map(shards, mesh=mesh, in_specs=in_specs, out_specs=out_specs, check_vma=False)
```

profile of v0, /device:TPU:1, one launch (start us, length us, event | category | flops | bytes accessed | tf_op | source)
XLA Modules:
  0.0 1061.4 jit_solution(15433672871197488146)
XLA Ops:
  7.2 0.7 convert_element_type.3
  8.0 0.9 reduce_sum.70
  8.9 1.0 multiply_reduce_fusion.1
  9.9 1.3 convolution_bitcast_fusion.2
  11.8 33.6 %all_to_all.108 = f32[16,1,1024]{2,1,0:T(1,128)S(1)} all-to-all(f32[16,1,1024]{2,1,0:T(1,128)S(1)} %reshape.79), channel_id=1, replica_groups=mesh['row'=32,'ch'=16] {'ch'}, dimensions={0} | all-to-all | bytes 131072 | tf_op jit(solution)/shard_map/all_to_all | solution.py:40
  45.3 0.5 broadcast.151
  45.9 0.8 reduce.3
  47.2 0.9 all_to_all.85
  48.6 17.4 %all_to_all.109 = f32[16,1,1024]{2,1,0:T(1,128)S(1)} all-to-all(f32[16,1,1024]{2,1,0:T(1,128)S(1)} %reshape.77), channel_id=1, replica_groups=mesh['row'=32,'ch'=16] {'ch'}, dimensions={0} | all-to-all | bytes 131072 | tf_op jit(solution)/shard_map/all_to_all | solution.py:39
  66.0 0.8 reduce.2
  67.6 179.4 %all-gather.2.cloned.1.call-done = f32[8,256,256]{2,1,0:T(8,128)} async-done(((f32[8,8,256]{2,1,0:T(8,128)}), f32[8,256,256]{2,1,0:T(8,128)}) %all-gather.2.cloned.1.call-update) | async-done | bytes 2097168 | tf_op jit(solution)/shard_map/all_gather | solution.py:42
  247.0 3.4 fusion.35
  250.4 0.4 copy.35
  250.8 1.2 reshape.81
  252.0 34.7 %all-to-all-start.2 = ((f32[16,1,1024]{2,1,0:T(1,128)}), f32[16,1,1024]{2,1,0:T(1,128)S(1)}, u32[]{:S(2)}, u32[]{:S(2)}) async-start(f32[16,1,1024]{2,1,0:T(1,128)} %reshape.81), calls=%async_computation.2 | async-start | bytes 131072 | tf_op jit(solution)/shard_map/all_to_all | solution.py:44
  287.1 14.2 %all-to-all-done.2 = f32[16,1,1024]{2,1,0:T(1,128)S(1)} async-done(((f32[16,1,1024]{2,1,0:T(1,128)}), f32[16,1,1024]{2,1,0:T(1,128)S(1)}, u32[]{:S(2)}, u32[]{:S(2)}) %all-to-all-start.2) | async-done | bytes 65568 | tf_op jit(solution)/shard_map/all_to_all | solution.py:44
  301.3 0.8 reduce.4
  302.1 0.6 reshape.82
  302.7 0.3 copy.36
  303.5 0.4 fusion.17
  304.8 17.8 %all_to_all.110 = f32[16,1,1024]{2,1,0:T(1,128)S(1)} all-to-all(f32[16,1,1024]{2,1,0:T(1,128)S(1)} %reshape.83), channel_id=1, replica_groups=mesh['row'=32,'ch'=16] {'ch'}, dimensions={0} | all-to-all | bytes 131072 | tf_op jit(solution)/shard_map/all_to_all | solution.py:49
  322.5 0.8 reduce.5
  324.1 1.9 convolution_bitcast_fusion
  326.0 2.0 copy.40
  328.0 1.6 copy-done.1
  329.5 1.1 fusion.36
  330.6 0.4 copy.45
  331.1 1.2 reshape.85
  332.2 3.7 all-to-all-start.5
  335.9 0.9 fusion.34
  336.8 201.7 %reduce-scatter.2.cloned.1.call-done = f32[8,8,256]{2,1,0:T(8,128)} async-done(((f32[256,8,256]{2,1,0:T(8,128)}), f32[8,8,256]{2,1,0:T(8,128)}) %reduce-scatter.2.cloned.1.call-update) | async-done | bytes 65552 | tf_op jit(solution)/shard_map/reduce_scatter | solution.py:51
  538.6 1.3 copy.41
  539.8 1.2 reshape.87
  541.0 32.8 %all-to-all-start.4 = ((f32[16,1,1024]{2,1,0:T(1,128)}), f32[16,1,1024]{2,1,0:T(1,128)S(1)}, u32[]{:S(2)}, u32[]{:S(2)}) async-start(f32[16,1,1024]{2,1,0:T(1,128)} %reshape.87), calls=%async_computation.5 | async-start | bytes 131072 | tf_op jit(solution)/shard_map/all_to_all | solution.py:60
  573.8 1.0 convolution_bitcast_fusion.3
  574.8 1.0 convolution_bitcast_fusion.4
  575.8 0.8 reduce.7
  576.6 0.6 reshape.86
  577.7 10.6 all-to-all-done.4
  588.3 0.8 reduce.6
  589.1 0.6 reshape.88
  590.4 0.4 fusion.5
  590.8 1.2 convolution_bitcast_fusion.1
  592.0 0.3 multiply_reduce_fusion
  592.6 0.8 broadcast_add_fusion
  593.3 458.3 %all-reduce.7.cloned.1.call-done = (f32[128,512]{1,0:T(8,128)}, f32[128,128]{1,0:T(8,128)}, f32[128,128]{1,0:T(8,128)}) async-done(((f32[128,512]{1,0:T(8,128)}, f32[128,128]{1,0:T(8,128)}, f32[128,128]{1,0:T(8,128)}), (f32[128,512]{1,0:T(8,128)}, f32[128,128]{1,0:T(8,128)}, f32[128,128]{1,0:T(8,128)})) %all-reduce.7.cloned.1.call-update) | async-done | bytes 393232 | tf_op jit(solution)/shard_map/psum | solution.py:63
  1051.6 1.7 broadcast_multiply_fusion
  1053.3 1.5 broadcast_multiply_fusion.1
  (53 shorter events, 6.2 us)
Async XLA Ops:
  7.2 2.8 copy-start
  7.2 239.8 %all-gather.2.cloned.1.call-start = ((), (), s32[]{:S(2)}) async-start(), calls=%async_computation.7 | async-start | bytes 2162688 | tf_op jit(solution)/shard_map/all_gather | solution.py:42
  67.6 219.2 %copy-start.2 = (f32[8,16,128]{2,1,0:T(8,128)S(1)}, f32[8,16,128]{2,1,0:T(8,128)}, u32[]{:S(2)}) copy-start(f32[8,16,128]{2,1,0:T(8,128)} %param.6) | copy-start | bytes 196612
  67.6 219.2 %copy-start.5 = (f32[128,128]{1,0:T(8,128)S(1)}, f32[128,128]{1,0:T(8,128)}, u32[]{:S(2)}) copy-start(f32[128,128]{1,0:T(8,128)} %param.9) | copy-start | bytes 196612
  252.0 49.3 %all-to-all-start.2 = ((f32[16,1,1024]{2,1,0:T(1,128)}), f32[16,1,1024]{2,1,0:T(1,128)S(1)}, u32[]{:S(2)}, u32[]{:S(2)}) async-start(f32[16,1,1024]{2,1,0:T(1,128)} %reshape.81), calls=%async_computation.2 | async-start | bytes 131072 | tf_op jit(solution)/shard_map/all_to_all | solution.py:44
  286.7 251.8 %reduce-scatter.2.cloned.1.call-start = ((), (), s32[]{:S(2)}) async-start(), calls=%async_computation.8 | async-start | bytes 2162688 | tf_op jit(solution)/shard_map/reduce_scatter | solution.py:51
  302.1 1.5 copy-start.3
  302.1 1.4 copy-start.4
  327.9 1.6 copy-start.1
  332.2 208.8 %all-to-all-start.5 = ((f32[16,1,1024]{2,1,0:T(1,128)}), f32[16,1,1024]{2,1,0:T(1,128)S(1)}, u32[]{:S(2)}, u32[]{:S(2)}) async-start(f32[16,1,1024]{2,1,0:T(1,128)} %reshape.85), calls=%async_computation.6 | async-start | bytes 131072 | tf_op jit(solution)/shard_map/all_to_all | solution.py:59
  541.0 47.3 %all-to-all-start.4 = ((f32[16,1,1024]{2,1,0:T(1,128)}), f32[16,1,1024]{2,1,0:T(1,128)S(1)}, u32[]{:S(2)}, u32[]{:S(2)}) async-start(f32[16,1,1024]{2,1,0:T(1,128)} %reshape.87), calls=%async_computation.5 | async-start | bytes 131072 | tf_op jit(solution)/shard_map/all_to_all | solution.py:60
  573.8 477.8 %all-reduce.7.cloned.1.call-start = ((), (), s32[]{:S(2)}) async-start(), calls=%async_computation.9 | async-start | bytes 786432 | tf_op jit(solution)/shard_map/psum | solution.py:63
Sparse Core Ops, SparseCore 0:
  48.2 198.7 all-gather.1
  328.1 210.4 reduce-scatter.1
  592.7 458.8 all-reduce.6
where the time goes:
time: 1060 us
  waiting for transfers between devices  864 us (82%)
  starting transfers between devices  71.4 us (7%)
  blocking collectives  68.8 us (6%)
  local copies, waits for them, and re-layouts  17.3 us (2%)
  between operations  14.1 us (1%)
  matrix products  13 us (1%)
  other arithmetic  12.5 us (1%)
    psum x1, waiting for transfers between devices, shards(): lax.psum((d_win, d_wgate, d_wout), ('row', 'ch'))  458 us
    reduce_scatter x1, waiting for transfers between devices, shards(): lax.psum_scatter(jnp.einsum('hij,hik->jhk', d_tri_c, left_c, precision=hi...  202 us
    all_gather x1, waiting for transfers between devices, shards(): right_all = lax.all_gather(right_c, 'row', axis=1, tiled=True)  179 us
    all_to_all x1, starting transfers between devices, shards(): lax.all_to_all(tri_c, 'ch', split_axis=2, concat_axis=0, tiled=True)  34.7 us
    all_to_all x1, blocking collectives, shards(): lax.all_to_all(right, 'ch', split_axis=0, concat_axis=2, tiled=True)  33.6 us
    all_to_all x1, starting transfers between devices, shards(): lax.all_to_all(d_right_c, 'ch', split_axis=2, concat_axis=0, tiled=True)  32.8 us
  transfers between devices with their start and end apart: 6, of which 5 were waited for; matrix products, arithmetic and copies ran while one was open for 1% of the time, Pallas kernels for 0%

commit v1 on v0

v1 whole, which is shorter than its diff:
```python
import jax
import jax.numpy as jnp
from jax import lax
from jax.experimental import pallas as pl
from jax.experimental.pallas import tpu as pltpu
from jax.sharding import Mesh, PartitionSpec as P

ROW = ("x", "zl")
CH = ("y", "zh", "co")
CHANNELS = ("zh", "co", "x", "zl")
PLANE = ("x", "y", "co")
DEPTH = ("zl", "zh")
F32 = jnp.float32
EPS = 1e-05


def dot(a, b, ca, cb):
    return lax.dot_general(
        a, b, (((ca,), (cb,)), ((), ())), precision=lax.Precision.HIGHEST, preferred_element_type=F32
    )


def call(body, outs, scratch=()):
    vmem = pl.BlockSpec(memory_space=pltpu.VMEM)

    def run(*args):
        return pl.pallas_call(
            body,
            out_shape=[jax.ShapeDtypeStruct(s, F32) for s in outs],
            in_specs=[vmem] * len(args),
            out_specs=[vmem] * len(outs),
            scratch_shapes=[pltpu.VMEM(s, F32) for s in scratch],
            compiler_params=pltpu.CompilerParams(vmem_limit_bytes=32 * 1024 * 1024),
        )(*args)

    return run


def norm_rows(values):
    center = values - jnp.mean(values, axis=1, keepdims=True)
    spread = jnp.mean(center * center, axis=1, keepdims=True)
    rstd = 1.0 / jnp.sqrt(spread + EPS)
    return center * rstd, rstd


def mask_lanes(mask_ref, lanes_ref):
    maskf = mask_ref[...].astype(F32)
    for ii in range(8):
        lanes_ref[0:1, ii * 16 : (ii + 1) * 16] = maskf[ii : ii + 1, :]
    return lanes_ref[0:1, :]


def enter_kernel(pair_ref, mask_ref, win_ref, wgate_ref, msg_ref, proj_ref, normed_ref, gate_ref, lanes_ref):
    normed, _ = norm_rows(pair_ref[...].reshape(128, 128))
    maskf = mask_lanes(mask_ref, lanes_ref)
    proj = dot(win_ref[...], normed, 0, 1)
    proj_ref[...] = proj
    msg_ref[:, 0, 0:128] = maskf * jax.nn.sigmoid(proj[0:128]) * proj[128:256]
    msg_ref[:, 0, 128:256] = maskf * jax.nn.sigmoid(proj[256:384]) * proj[384:512]
    normed_ref[...] = normed
    gate_ref[...] = jax.nn.sigmoid(dot(normed, wgate_ref[...], 1, 0))


def triangle_kernel(msg_ref, part_ref, left_ref, right_ref, flat_ref, turn_ref):
    flat_ref[...] = msg_ref[:, 0, :]
    for s in range(8):
        rows = slice(s * 32, (s + 1) * 32)
        for q in range(4):
            block = flat_ref[q * 32 : (q + 1) * 32, s * 16 : (s + 1) * 16]
            left_ref[rows, q * 16 : (q + 1) * 16] = block
            block = flat_ref[q * 32 : (q + 1) * 32, 128 + s * 16 : 128 + (s + 1) * 16]
            turn_ref[rows, q * 16 : (q + 1) * 16] = block
        right_ref[pl.ds(s, 32, stride=8), :] = turn_ref[rows, :]
    part_ref[...] = dot(right_ref[...], left_ref[...], 1, 1).reshape(4, 64, 256)


def home_kernel(part_ref, msg_ref, flat_ref):
    total = ((part_ref[0] + part_ref[1]) + (part_ref[2] + part_ref[3])).T
    for q in range(4):
        for s in range(8):
            flat_ref[q * 32 : (q + 1) * 32, s * 16 : (s + 1) * 16] = total[
                s * 32 : (s + 1) * 32, q * 16 : (q + 1) * 16
            ]
    msg_ref[:, 0, :] = flat_ref[...]


def norm_channels(values):
    center = values - jnp.mean(values, axis=0, keepdims=True)
    spread = jnp.mean(center * center, axis=0, keepdims=True)
    rstd = 1.0 / jnp.sqrt(spread + EPS)
    return center * rstd, rstd


def turn_kernel(tri_ref, cot_ref, gate_ref, wout_ref, msg_ref):
    normed, rstd = norm_channels(tri_ref[:, 0, :])
    d_out = cot_ref[...].reshape(128, 128) * gate_ref[...]
    d_normed = dot(wout_ref[...], d_out, 1, 1)
    along = jnp.mean(d_normed * normed, axis=0, keepdims=True)
    msg_ref[:, 0, :] = rstd * (d_normed - jnp.mean(d_normed, axis=0, keepdims=True) - normed * along)


def update_kernel(tri_ref, cot_ref, gate_ref, normed_ref, wgate_ref, wout_ref, upd_ref, dn_ref, dwg_ref, dwo_ref):
    normed_tri, _ = norm_channels(tri_ref[:, 0, :])
    gate = gate_ref[...]
    cot = cot_ref[...].reshape(128, 128)
    out_proj = dot(normed_tri, wout_ref[...], 0, 0)
    upd_ref[...] = (gate * out_proj).reshape(8, 16, 128)
    dwo_ref[...] = dot(normed_tri, cot * gate, 1, 0)
    d_pre = cot * out_proj * gate * (1.0 - gate)
    dwg_ref[...] = dot(normed_ref[...], d_pre, 0, 0)
    dn_ref[...] = dot(d_pre, wgate_ref[...], 1, 1)


def spread_kernel(msg_ref, out_ref, flat_ref, whole_ref):
    flat_ref[...] = msg_ref[:, 0, :]
    for q in range(4):
        for s in range(8):
            whole_ref[s * 32 : (s + 1) * 32, q * 16 : (q + 1) * 16] = flat_ref[
                q * 32 : (q + 1) * 32, s * 16 : (s + 1) * 16
            ]
    turned = whole_ref[...].T
    for y in range(4):
        out_ref[y] = turned


def back_kernel(dtri_ref, left_ref, right_ref, msg_ref, flat_ref, dright_ref):
    dtri = dtri_ref[...].reshape(256, 256)
    d_left = dot(dtri, right_ref[...], 0, 0)
    dright_ref[...] = dot(dtri, left_ref[...], 1, 0)
    for s in range(8):
        d_right = dright_ref[pl.ds(s, 32, stride=8), :]
        for q in range(4):
            rows, lanes = slice(q * 32, (q + 1) * 32), slice(q * 16, (q + 1) * 16)
            flat_ref[rows, s * 16 : (s + 1) * 16] = d_left[s * 32 : (s + 1) * 32, lanes]
            flat_ref[rows, 128 + s * 16 : 128 + (s + 1) * 16] = d_right[:, lanes]
    msg_ref[:, 0, :] = flat_ref[...]


def leave_kernel(
    msg_ref, proj_ref, pair_ref, mask_ref, win_ref, dn_ref, dwg_ref, dwo_ref, dpair_ref, weights_ref, dproj_ref, lanes_ref
):
    normed, rstd = norm_rows(pair_ref[...].reshape(128, 128))
    maskf = mask_lanes(mask_ref, lanes_ref)
    for side in range(2):
        base = side * 256
        d_side = maskf * msg_ref[:, 0, side * 128 : (side + 1) * 128]
        sig = jax.nn.sigmoid(proj_ref[base : base + 128])
        d_value = d_side * sig
        dproj_ref[base : base + 128] = d_value * proj_ref[base + 128 : base + 256] * (1.0 - sig)
        dproj_ref[base + 128 : base + 256] = d_value
    d_proj = dproj_ref[...]
    weights_ref[0:512] = dot(d_proj, normed, 1, 0)
    weights_ref[512:640] = dwg_ref[...]
    weights_ref[640:768] = dwo_ref[...]
    d_normed = dot(d_proj, win_ref[...], 0, 1) + dn_ref[...]
    along = jnp.mean(d_normed * normed, axis=1, keepdims=True)
    d_pair = rstd * (d_normed - jnp.mean(d_normed, axis=1, keepdims=True) - normed * along)
    dpair_ref[...] = d_pair.reshape(8, 16, 128)


def sum_kernel(scale, parts_ref, out_ref):
    total = jnp.sum(parts_ref[...], axis=0) * scale
    for i in range(out_ref.shape[0]):
        out_ref[i] = total


def unpack_kernel(parts_ref, dwin_ref, dwg_ref, dwo_ref):
    whole = parts_ref[...].reshape(768, 128)
    dwin_ref[...] = whole[0:512].T
    dwg_ref[...] = whole[512:640]
    dwo_ref[...] = whole[640:768]


def swap(values, axes):
    return lax.all_to_all(values, axes, split_axis=0, concat_axis=0, tiled=True)


def shards(pair, pair_mask, w_in, w_gate, w_out, cotangent):
    msg, proj, normed, gate = call(
        enter_kernel, [(128, 1, 256), (512, 128), (128, 128), (128, 128)], [(8, 128)]
    )(pair, pair_mask, w_in, w_gate)
    msg = swap(msg, CHANNELS)
    part, left, right = call(triangle_kernel, [(4, 64, 256), (256, 64), (256, 64)], [(128, 256), (256, 64)])(msg)
    part = swap(part, "y")
    (msg,) = call(home_kernel, [(128, 1, 128)], [(128, 128)])(part)
    tri = swap(msg, CHANNELS)
    (msg,) = call(turn_kernel, [(128, 1, 128)])(tri, cotangent, gate, w_out)
    msg = swap(msg, CHANNELS)
    update, d_normed, d_wgate, d_wout = call(
        update_kernel, [(8, 16, 128), (128, 128), (128, 128), (128, 128)]
    )(tri, cotangent, gate, normed, w_gate, w_out)
    (d_tri,) = call(spread_kernel, [(4, 64, 256)], [(128, 128), (256, 64)])(msg)
    d_tri = swap(d_tri, "y")
    (msg,) = call(back_kernel, [(128, 1, 256)], [(128, 256), (256, 64)])(d_tri, left, right)
    msg = swap(msg, CHANNELS)
    d_pair, weights = call(
        leave_kernel, [(8, 16, 128), (768, 128)], [(512, 128), (8, 128)]
    )(msg, proj, pair, pair_mask, w_in, d_normed, d_wgate, d_wout)
    parts = swap(weights.reshape(32, 24, 128), PLANE)
    (parts,) = call(lambda a, b: sum_kernel(1.0, a, b), [(16, 24, 128)])(parts)
    parts = swap(parts, DEPTH)
    scale = 1.0 / (pair.shape[0] * lax.axis_size(ROW))
    (parts,) = call(lambda a, b: sum_kernel(scale, a, b), [(32, 24, 128)])(parts)
    parts = swap(parts, PLANE)
    d_win, d_wgate, d_wout = call(unpack_kernel, [(128, 512), (128, 128), (128, 128)])(parts)
    return (update, d_pair, d_win, d_wgate, d_wout)


def solution(mesh):
    fine = Mesh(mesh.devices.reshape(4, 8, 4, 2, 2), ("x", "zl", "y", "zh", "co"))
    in_specs = (P(ROW, CH, None), P(ROW, CH), P(), P(), P(), P(ROW, CH, None))
    out_specs = (P(ROW, CH, None), P(ROW, CH, None), P(), P(), P())
    return jax.shard_map(shards, mesh=fine, in_specs=in_specs, out_specs=out_specs, check_vma=False)
```

time: 1060 us -> 185 us (0.17)
  waiting for transfers between devices: 864 us -> 17.5 us
  blocking collectives: 68.8 us -> 149 us
  starting transfers between devices: 71.4 us -> 6.75 us
  local copies, waits for them, and re-layouts: 17.3 us -> 3.34 us
  between operations: 14.1 us -> 0.75 us
  matrix products: 13 us -> 0 us
  other arithmetic: 12.5 us -> 0 us
    psum x1 -> x0, waiting for transfers between devices: 458 us -> none  [shards(): lax.psum((d_win, d_wgate, d_wout), ('row', 'ch'))]
    reduce_scatter x1 -> x0, waiting for transfers between devices: 202 us -> none  [shards(): lax.psum_scatter(jnp.einsum('hij,hik->jhk', d_tri_c, left_c, precision=hi...]
    all_gather x1 -> x0, waiting for transfers between devices: 179 us -> none  [shards(): right_all = lax.all_gather(right_c, 'row', axis=1, tiled=True)]
    all_to_all x3 -> x8, blocking collectives: 68.8 us -> 149 us  [swap(): return lax.all_to_all(values, axes, split_axis=0, concat_axis=0, tiled=True)]
    all_to_all x3 -> x1, starting transfers between devices: 71.3 us -> 6.75 us  [swap(): return lax.all_to_all(values, axes, split_axis=0, concat_axis=0, tiled=True)]
    dot_general x12 -> x0, matrix products: 13 us -> none  [the longest x1 3.38 us: shards(): tri_c = jnp.einsum('hik,hjk->hij', left_c, right_all, precision=highest)]
    all_to_all x3 -> x1, waiting for transfers between devices: 24.8 us -> 17.5 us  [swap(): return lax.all_to_all(values, axes, split_axis=0, concat_axis=0, tiled=True)]
  transfers between devices with their start and end apart: 6 -> 1, of which waited for: 5 -> 1; matrix products, arithmetic and copies ran while one was open for 1% -> 0% of each run, Pallas kernels for 0% -> 1%
where the time goes in v1:
time: 185 us; the launch traced here: 184 us
  blocking collectives  149 us (81%)
  waiting for transfers between devices  17.5 us (9%)
  Pallas kernels  7.23 us (4%)
  starting transfers between devices  6.75 us (4%)
  local copies, waits for them, and re-layouts  3.34 us (2%)
    all_to_all x8, blocking collectives, swap(): return lax.all_to_all(values, axes, split_axis=0, concat_axis=0, tiled=True)  149 us
    all_to_all x1, waiting for transfers between devices, swap(): return lax.all_to_all(values, axes, split_axis=0, concat_axis=0, tiled=True)  17.5 us
    pallas_call x11, Pallas kernels, run(): pl.pallas_call(body, out_shape=[jax.ShapeDtypeStruct(s, F32) for s in out...  7.23 us
    all_to_all x1, starting transfers between devices, swap(): return lax.all_to_all(values, axes, split_axis=0, concat_axis=0, tiled=True)  6.75 us
  transfers between devices with their start and end apart: 1, of which 1 were waited for; matrix products, arithmetic and copies ran while one was open for 0% of the time, Pallas kernels for 1%

profile of v1, /device:TPU:1, one launch (start us, length us, event | category | flops | bytes accessed | tf_op | source)
XLA Modules:
  0.0 184.3 jit_solution(10781010643810493882)
XLA Ops:
  0.6 0.0 copy-start
  0.6 0.9 copy-done
  1.6 0.0 copy-start.2
  1.6 0.8 copy-done.2
  2.4 0.0 copy-start.4
  2.4 0.8 copy-done.4
  3.3 0.0 copy-start.8
  3.3 0.7 copy-done.8
  4.0 0.6 shard_map.101
  4.6 38.9 %all_to_all.45.msg_ref = f32[128,1,256]{2,1,0:T(1,128)S(1)} all-to-all(f32[128,1,256]{2,1,0:T(1,128)S(1)} %get-tuple-element.21), channel_id=1, replica_groups=mesh['x'=4,'zl'=8,'y'=4,'zh'=2,'co'=2] {'zh','co','x','zl'}, dimensions={0} | all-to-all | bytes 262144 | tf_op jit(solution)/shard_map/all_to_all | solution.py:175
  43.5 0.7 shard_map.102
  44.2 9.8 %all_to_all.46.part_ref = f32[4,64,256]{2,1,0:T(8,128)S(1)} all-to-all(f32[4,64,256]{2,1,0:T(8,128)S(1)} %get-tuple-element.22), channel_id=1, replica_groups=mesh['x'=4,'zl'=8,'y'=4,'zh'=2,'co'=2] {'y'}, dimensions={0} | all-to-all | bytes 524288 | tf_op jit(solution)/shard_map/all_to_all | solution.py:175
  54.0 0.3 shard_map.103
  54.3 0.0 copy-start.6
  54.3 0.0 copy-start.7
  54.4 22.4 %all_to_all.47.tri_ref = f32[128,1,128]{2,1,0:T(1,128)S(1)} all-to-all(f32[128,1,128]{2,1,0:T(1,128)S(1)} %shard_map.103), channel_id=1, replica_groups=mesh['x'=4,'zl'=8,'y'=4,'zh'=2,'co'=2] {'zh','co','x','zl'}, dimensions={0} | all-to-all | bytes 131072 | tf_op jit(solution)/shard_map/all_to_all | solution.py:175
  76.8 0.0 copy-done.6
  76.8 0.0 copy-done.7
  76.8 0.3 shard_map.105
  77.1 20.9 %all_to_all.48.msg_ref = f32[128,1,128]{2,1,0:T(1,128)S(1)} all-to-all(f32[128,1,128]{2,1,0:T(1,128)S(1)} %shard_map.105), channel_id=1, replica_groups=mesh['x'=4,'zl'=8,'y'=4,'zh'=2,'co'=2] {'zh','co','x','zl'}, dimensions={0} | all-to-all | bytes 131072 | tf_op jit(solution)/shard_map/all_to_all | solution.py:175
  98.0 0.3 shard_map.106
  98.3 8.8 %all_to_all.49.dtri_ref = f32[4,64,256]{2,1,0:T(8,128)S(1)} all-to-all(f32[4,64,256]{2,1,0:T(8,128)S(1)} %shard_map.106), channel_id=1, replica_groups=mesh['x'=4,'zl'=8,'y'=4,'zh'=2,'co'=2] {'y'}, dimensions={0} | all-to-all | bytes 524288 | tf_op jit(solution)/shard_map/all_to_all | solution.py:175
  107.1 1.5 shard_map.107
  108.6 0.0 copy-start.5
  108.6 6.7 %all-to-all-start.5 = ((f32[128,1,256]{2,1,0:T(1,128)}), f32[128,1,256]{2,1,0:T(1,128)S(1)}, u32[]{:S(2)}, u32[]{:S(2)}) async-start(f32[128,1,256]{2,1,0:T(1,128)} %shard_map.107), calls=%async_computation.5 | async-start | bytes 262144 | tf_op jit(solution)/shard_map/all_to_all | solution.py:175
  115.4 0.0 copy-start.1
  115.4 0.0 copy-done.5
  115.4 0.0 copy-start.3
  115.4 1.1 shard_map.104
  116.5 0.0 copy-start.9
  116.5 17.5 %all-to-all-done.5.msg_ref = f32[128,1,256]{2,1,0:T(1,128)S(1)} async-done(((f32[128,1,256]{2,1,0:T(1,128)}), f32[128,1,256]{2,1,0:T(1,128)S(1)}, u32[]{:S(2)}, u32[]{:S(2)}) %all-to-all-start.5) | async-done | bytes 131104 | tf_op jit(solution)/shard_map/all_to_all | solution.py:175
  134.0 0.0 copy-done.1
  134.0 0.0 copy-done.3
  134.0 0.0 copy-done.9
  134.0 1.5 shard_map.108
  135.5 13.9 %all_to_all.50.a = f32[32,24,128]{2,1,0:T(8,128)S(1)} all-to-all(f32[32,24,128]{2,1,0:T(8,128)S(1)} %bitcast.1), channel_id=1, replica_groups=mesh['x'=4,'zl'=8,'y'=4,'zh'=2,'co'=2] {'x','y','co'}, dimensions={0} | all-to-all | bytes 786432 | tf_op jit(solution)/shard_map/all_to_all | solution.py:175
  149.4 17.7 %all_to_all.51.a = f32[16,24,128]{2,1,0:T(8,128)S(1)} all-to-all(f32[16,24,128]{2,1,0:T(8,128)S(1)} %shard_map.109), channel_id=1, replica_groups=mesh['x'=4,'zl'=8,'y'=4,'zh'=2,'co'=2] {'zl','zh'}, dimensions={0} | all-to-all | bytes 393216 | tf_op jit(solution)/shard_map/all_to_all | solution.py:175
  167.2 16.3 %all_to_all.52.parts_ref = f32[32,24,128]{2,1,0:T(8,128)S(1)} all-to-all(f32[32,24,128]{2,1,0:T(8,128)S(1)} %shard_map.110), channel_id=1, replica_groups=mesh['x'=4,'zl'=8,'y'=4,'zh'=2,'co'=2] {'x','y','co'}, dimensions={0} | all-to-all | bytes 786432 | tf_op jit(solution)/shard_map/all_to_all | solution.py:175
  183.5 0.8 shard_map.111
  (2 shorter events, 0.1 us)
Async XLA Ops:
  0.6 1.0 copy-start
  1.6 0.8 copy-start.2
  2.4 0.8 copy-start.4
  3.3 0.7 copy-start.8
  54.3 22.4 %copy-start.6 = (f32[8,16,128]{2,1,0:T(8,128)S(1)}, f32[8,16,128]{2,1,0:T(8,128)}, u32[]{:S(2)}) copy-start(f32[8,16,128]{2,1,0:T(8,128)} %cot_ref.3) | copy-start | bytes 196612
  54.3 22.4 %copy-start.7 = (f32[128,128]{1,0:T(8,128)S(1)}, f32[128,128]{1,0:T(8,128)}, u32[]{:S(2)}) copy-start(f32[128,128]{1,0:T(8,128)} %wout_ref.3) | copy-start | bytes 196612
  108.6 6.8 %copy-start.5 = (f32[128,128]{1,0:T(8,128)S(1)}, f32[128,128]{1,0:T(8,128)}, u32[]{:S(2)}) copy-start(f32[128,128]{1,0:T(8,128)} %wgate_ref.3) | copy-start | bytes 196612
  108.6 25.4 %all-to-all-start.5 = ((f32[128,1,256]{2,1,0:T(1,128)}), f32[128,1,256]{2,1,0:T(1,128)S(1)}, u32[]{:S(2)}, u32[]{:S(2)}) async-start(f32[128,1,256]{2,1,0:T(1,128)} %shard_map.107), calls=%async_computation.5 | async-start | bytes 262144 | tf_op jit(solution)/shard_map/all_to_all | solution.py:175
  115.4 18.6 %copy-start.1 = (f32[128,512]{1,0:T(8,128)S(1)}, f32[128,512]{1,0:T(8,128)}, u32[]{:S(2)}) copy-start(f32[128,512]{1,0:T(8,128)} %win_ref.3) | copy-start | bytes 786436
  115.4 18.6 %copy-start.3 = (f32[8,16,128]{2,1,0:T(8,128)S(1)}, f32[8,16,128]{2,1,0:T(8,128)}, u32[]{:S(2)}) copy-start(f32[8,16,128]{2,1,0:T(8,128)} %pair_ref.3) | copy-start | bytes 196612
  116.5 17.5 %copy-start.9 = (s32[8,16]{1,0:T(8,128)S(1)}, s32[8,16]{1,0:T(8,128)}, u32[]{:S(2)}) copy-start(s32[8,16]{1,0:T(8,128)} %mask_ref.3) | copy-start | bytes 1540

commit v2 on v1

v2 whole, which is shorter than its diff:
```python
import jax
import jax.numpy as jnp
from jax import lax
from jax.experimental import pallas as pl
from jax.experimental.pallas import tpu as pltpu
from jax.sharding import Mesh, PartitionSpec as P

ROW = ("x", "zl")
CH = ("y", "zh", "co")
CHANNELS = ("co", "x", "zl", "zh")
HOMES = ("x", "zl", "zh")
COLUMNS = ("y", "co")
PLANE = ("x", "y", "co")
DEPTH = ("zl", "zh")
F32 = jnp.float32
EPS = 1e-05


def dot(a, b, ca, cb):
    return lax.dot_general(
        a, b, (((ca,), (cb,)), ((), ())), precision=lax.Precision.HIGHEST, preferred_element_type=F32
    )


def call(body, outs, scratch=()):
    vmem = pl.BlockSpec(memory_space=pltpu.VMEM)

    def run(*args):
        return pl.pallas_call(
            body,
            out_shape=[jax.ShapeDtypeStruct(s, F32) for s in outs],
            in_specs=[vmem] * len(args),
            out_specs=[vmem] * len(outs),
            scratch_shapes=[pltpu.VMEM(s, F32) for s in scratch],
            compiler_params=pltpu.CompilerParams(vmem_limit_bytes=32 * 1024 * 1024),
        )(*args)

    return run


def norm_rows(values):
    center = values - jnp.mean(values, axis=1, keepdims=True)
    spread = jnp.mean(center * center, axis=1, keepdims=True)
    rstd = 1.0 / jnp.sqrt(spread + EPS)
    return center * rstd, rstd


def mask_lanes(mask_ref, lanes_ref):
    maskf = mask_ref[...].astype(F32)
    for ii in range(8):
        lanes_ref[0:1, ii * 16 : (ii + 1) * 16] = maskf[ii : ii + 1, :]
    return lanes_ref[0:1, :]


def enter_kernel(
    pair_hbm, mask_hbm, win_hbm, wgate_hbm, msg_ref, proj_ref, normed_ref, gate_ref,
    lanes_ref, pair_ref, mask_ref, win_ref, wgate_ref, sems
):
    sources = (pair_hbm, mask_hbm, win_hbm, wgate_hbm)
    copies = [
        pltpu.make_async_copy(source, target, sems.at[i])
        for i, (source, target) in enumerate(zip(sources, (pair_ref, mask_ref, win_ref, wgate_ref)))
    ]
    for copy in copies:
        copy.start()
    copies[0].wait()
    normed, _ = norm_rows(pair_ref[...].reshape(128, 128))
    normed_ref[...] = normed
    copies[1].wait()
    maskf = mask_lanes(mask_ref, lanes_ref)
    copies[2].wait()
    proj = dot(win_ref[...], normed, 0, 1)
    proj_ref[...] = proj
    msg_ref[:, 0, 0:128] = maskf * jax.nn.sigmoid(proj[0:128]) * proj[128:256]
    msg_ref[:, 0, 128:256] = maskf * jax.nn.sigmoid(proj[256:384]) * proj[384:512]
    copies[3].wait()
    gate_ref[...] = jax.nn.sigmoid(dot(normed, wgate_ref[...], 1, 0))


def column_blocks():
    return [
        (y * 64 + co * 32 + zh * 16, y * 64 + zh * 32 + co * 16) for y in range(4) for co in range(2) for zh in range(2)
    ]


def triangle_kernel(msg_ref, part_ref, left_ref, right_ref, flat_ref, turn_ref, natural_ref):
    flat_ref[0] = msg_ref[:, 0, 0:128]
    flat_ref[1] = msg_ref[:, 0, 128:256]
    for co in range(2):
        for zh in range(2):
            source, lanes = pl.ds(co * 64 + zh, 32, stride=2), slice(zh * 32 + co * 16, zh * 32 + co * 16 + 16)
            left, right = flat_ref[0, source, :], flat_ref[1, source, :]
            for s in range(8):
                rows = slice(s * 32, (s + 1) * 32)
                left_ref[rows, lanes] = left[:, s * 16 : (s + 1) * 16]
                turn_ref[rows, lanes] = right[:, s * 16 : (s + 1) * 16]
    for s in range(8):
        natural_ref[pl.ds(s, 32, stride=8), :] = turn_ref[s * 32 : (s + 1) * 32, :]
    for to, at in column_blocks():
        right_ref[to : to + 16, :] = natural_ref[at : at + 16, :]
    part_ref[...] = dot(right_ref[...], left_ref[...], 1, 1).reshape(8, 32, 256)


def home_kernel(part_ref, msg_ref, flat_ref, turn_ref):
    for h in range(2):
        total = ((part_ref[h] + part_ref[h + 2]) + (part_ref[h + 4] + part_ref[h + 6])).T
        for zh in range(2):
            for s in range(8):
                turn_ref[h, zh, :, s * 16 : (s + 1) * 16] = total[s * 32 : (s + 1) * 32, zh * 16 : (zh + 1) * 16]
            flat_ref[h, pl.ds(zh, 32, stride=2), :] = turn_ref[h, zh]
        msg_ref[:, 0, h * 128 : (h + 1) * 128] = flat_ref[h]


def gather_channels(msg_ref):
    return jnp.concatenate([msg_ref[:, 0, 0:128], msg_ref[:, 0, 128:256]], axis=0)


def norm_channels(values):
    center = values - jnp.mean(values, axis=0, keepdims=True)
    spread = jnp.mean(center * center, axis=0, keepdims=True)
    rstd = 1.0 / jnp.sqrt(spread + EPS)
    return center * rstd, rstd


def turn_kernel(tri_ref, cot_ref, gate_ref, wout_ref, msg_ref):
    normed, rstd = norm_channels(gather_channels(tri_ref))
    d_out = cot_ref[...].reshape(128, 128) * gate_ref[...]
    d_normed = dot(wout_ref[...], d_out, 1, 1)
    along = jnp.mean(d_normed * normed, axis=0, keepdims=True)
    d_tri = rstd * (d_normed - jnp.mean(d_normed, axis=0, keepdims=True) - normed * along)
    for h in range(2):
        msg_ref[:, 0, h * 128 : (h + 1) * 128] = d_tri[h * 64 : (h + 1) * 64]


def spread_kernel(msg_ref, out_ref, flat_ref, whole_ref):
    for h in range(2):
        flat_ref[h] = msg_ref[:, 0, h * 128 : (h + 1) * 128]
        for zh in range(2):
            block = flat_ref[h, pl.ds(zh, 32, stride=2), :]
            for s in range(8):
                whole_ref[h, s * 32 : (s + 1) * 32, zh * 16 : (zh + 1) * 16] = block[:, s * 16 : (s + 1) * 16]
        turned = whole_ref[h].T
        for y in range(4):
            out_ref[y * 2 + h] = turned


def back_kernel(dtri_ref, left_ref, right_ref, msg_ref, flat_ref, blocks_ref, natural_ref, turn_ref):
    dtri = dtri_ref[...].reshape(256, 256)
    blocks_ref[...] = dot(dtri, left_ref[...], 1, 0)
    d_left = dot(dtri, right_ref[...], 0, 0)
    for at, to in column_blocks():
        natural_ref[to : to + 16, :] = blocks_ref[at : at + 16, :]
    for s in range(8):
        d_right = natural_ref[pl.ds(s, 32, stride=8), :]
        for co in range(2):
            for zh in range(2):
                lanes = slice(zh * 32 + co * 16, zh * 32 + co * 16 + 16)
                turn_ref[0, co, zh, :, s * 16 : (s + 1) * 16] = d_left[s * 32 : (s + 1) * 32, lanes]
                turn_ref[1, co, zh, :, s * 16 : (s + 1) * 16] = d_right[:, lanes]
    for side in range(2):
        for co in range(2):
            for zh in range(2):
                flat_ref[side, pl.ds(co * 64 + zh, 32, stride=2), :] = turn_ref[side, co, zh]
        msg_ref[:, 0, side * 128 : (side + 1) * 128] = flat_ref[side]


def weights_kernel(
    msg_ref, proj_ref, normed_ref, mask_ref, tri_ref, cot_ref, gate_ref, wout_ref,
    weights_ref, dproj_ref, dpre_ref, out_ref, lanes_ref
):
    maskf = mask_lanes(mask_ref, lanes_ref)
    normed = normed_ref[...]
    normed_tri, _ = norm_channels(gather_channels(tri_ref))
    gate = gate_ref[...]
    cot = cot_ref[...].reshape(128, 128)
    out_proj = dot(normed_tri, wout_ref[...], 0, 0)
    out_ref[...] = out_proj
    d_pre = cot * out_proj * gate * (1.0 - gate)
    dpre_ref[...] = d_pre
    weights_ref[512:640] = dot(normed, d_pre, 0, 0)
    weights_ref[640:768] = dot(normed_tri, cot * gate, 1, 0)
    for side in range(2):
        base = side * 256
        d_side = maskf * msg_ref[:, 0, side * 128 : (side + 1) * 128]
        sig = jax.nn.sigmoid(proj_ref[base : base + 128])
        d_value = d_side * sig
        d_gate = d_value * proj_ref[base + 128 : base + 256] * (1.0 - sig)
        dproj_ref[base : base + 128] = d_gate
        dproj_ref[base + 128 : base + 256] = d_value
        weights_ref[base : base + 128] = dot(normed, d_gate, 0, 1)
        weights_ref[base + 128 : base + 256] = dot(normed, d_value, 0, 1)


def leave_kernel(dproj_ref, dpre_ref, out_ref, gate_ref, pair_ref, win_ref, wgate_ref, dpair_ref, upd_ref):
    upd_ref[...] = (gate_ref[...] * out_ref[...]).reshape(8, 16, 128)
    normed, rstd = norm_rows(pair_ref[...].reshape(128, 128))
    d_normed = dot(dproj_ref[...], win_ref[...], 0, 1) + dot(dpre_ref[...], wgate_ref[...], 1, 1)
    along = jnp.mean(d_normed * normed, axis=1, keepdims=True)
    d_pair = rstd * (d_normed - jnp.mean(d_normed, axis=1, keepdims=True) - normed * along)
    dpair_ref[...] = d_pair.reshape(8, 16, 128)


def sum_kernel(scale, parts_ref, out_ref):
    total = jnp.sum(parts_ref[...], axis=0) * scale
    for i in range(out_ref.shape[0]):
        out_ref[i] = total


def unpack_kernel(parts_ref, dwin_ref, dwg_ref, dwo_ref):
    whole = parts_ref[...].reshape(768, 128)
    for f in range(4):
        dwin_ref[:, f * 128 : (f + 1) * 128] = whole[f * 128 : (f + 1) * 128]
    dwg_ref[...] = whole[512:640]
    dwo_ref[...] = whole[640:768]


def swap(values, axes):
    return lax.all_to_all(values, axes, split_axis=0, concat_axis=0, tiled=True)


def enter(pair, pair_mask, w_in, w_gate):
    vmem = pl.BlockSpec(memory_space=pltpu.VMEM)
    outs = [(128, 1, 256), (512, 128), (128, 128), (128, 128)]
    return pl.pallas_call(
        enter_kernel,
        out_shape=[jax.ShapeDtypeStruct(s, F32) for s in outs],
        in_specs=[pl.BlockSpec(memory_space=pl.ANY)] * 4,
        out_specs=[vmem] * 4,
        scratch_shapes=[
            pltpu.VMEM((8, 128), F32),
            pltpu.VMEM(pair.shape, F32),
            pltpu.VMEM(pair_mask.shape, pair_mask.dtype),
            pltpu.VMEM(w_in.shape, F32),
            pltpu.VMEM(w_gate.shape, F32),
            pltpu.SemaphoreType.DMA((4,)),
        ],
        compiler_params=pltpu.CompilerParams(vmem_limit_bytes=60 * 1024 * 1024),
    )(pair, pair_mask, w_in, w_gate)


def shards(pair, pair_mask, w_in, w_gate, w_out, cotangent):
    msg, proj, normed, gate = enter(pair, pair_mask, w_in, w_gate)
    msg = swap(msg, CHANNELS)
    part, left, right = call(
        triangle_kernel, [(8, 32, 256), (256, 64), (256, 64)], [(2, 128, 128), (256, 64), (256, 64)]
    )(msg)
    part = swap(part, COLUMNS)
    (msg,) = call(home_kernel, [(64, 1, 256)], [(2, 64, 128), (2, 2, 32, 128)])(part)
    tri = swap(msg, HOMES)
    (msg,) = call(turn_kernel, [(64, 1, 256)])(tri, cotangent, gate, w_out)
    msg = swap(msg, HOMES)
    (d_tri,) = call(spread_kernel, [(8, 32, 256)], [(2, 64, 128), (2, 256, 32)])(msg)
    d_tri = swap(d_tri, COLUMNS)
    (msg,) = call(
        back_kernel, [(128, 1, 256)], [(2, 128, 128), (256, 64), (256, 64), (2, 2, 2, 32, 128)]
    )(d_tri, left, right)
    msg = swap(msg, CHANNELS)
    weights, d_proj, d_pre, out_proj = call(
        weights_kernel, [(768, 128), (512, 128), (128, 128), (128, 128)], [(8, 128)]
    )(msg, proj, normed, pair_mask, tri, cotangent, gate, w_out)
    parts = swap(weights.reshape(32, 24, 128), PLANE)
    d_pair, update = call(leave_kernel, [(8, 16, 128), (8, 16, 128)])(
        d_proj, d_pre, out_proj, gate, pair, w_in, w_gate
    )
    (parts,) = call(lambda a, b: sum_kernel(1.0, a, b), [(16, 24, 128)])(parts)
    parts = swap(parts, DEPTH)
    scale = 1.0 / (pair.shape[0] * lax.axis_size(ROW))
    (parts,) = call(lambda a, b: sum_kernel(scale, a, b), [(32, 24, 128)])(parts)
    parts = swap(parts, PLANE)
    d_win, d_wgate, d_wout = call(unpack_kernel, [(128, 512), (128, 128), (128, 128)])(parts)
    return (update, d_pair, d_win, d_wgate, d_wout)


def solution(mesh):
    fine = Mesh(mesh.devices.reshape(4, 8, 4, 2, 2), ("x", "zl", "y", "zh", "co"))
    in_specs = (P(ROW, CH, None), P(ROW, CH), P(), P(), P(), P(ROW, CH, None))
    out_specs = (P(ROW, CH, None), P(ROW, CH, None), P(), P(), P())
    return jax.shard_map(shards, mesh=fine, in_specs=in_specs, out_specs=out_specs, check_vma=False)
```

time: 185 us -> 180 us (0.973)
  waiting for transfers between devices: 17.5 us -> 9.11 us
  blocking collectives: 149 us -> 154 us
  local copies, waits for them, and re-layouts: 3.34 us -> 0.04 us
    all_to_all x1, waiting for transfers between devices: 17.5 us -> 9.11 us  [swap(): return lax.all_to_all(values, axes, split_axis=0, concat_axis=0, tiled=True)]
    all_to_all x8, blocking collectives: 149 us -> 154 us  [swap(): return lax.all_to_all(values, axes, split_axis=0, concat_axis=0, tiled=True)]
    unnamed x20 -> x18, local copies, waits for them, and re-layouts: 3.34 us -> 0.04 us
    pallas_call x0 -> x1, Pallas kernels: none -> 2.52 us  [enter(): pl.pallas_call(enter_kernel, out_shape=[jax.ShapeDtypeStruct(s, F32) for...]
    pallas_call x11 -> x10, Pallas kernels: 7.23 us -> 6.53 us  [run(): pl.pallas_call(body, out_shape=[jax.ShapeDtypeStruct(s, F32) for s in out...]
where the time goes in v2:
time: 180 us
  blocking collectives  154 us (86%)
  waiting for transfers between devices  9.11 us (5%)
  Pallas kernels  9.06 us (5%)
  starting transfers between devices  6.32 us (4%)
    all_to_all x8, blocking collectives, swap(): return lax.all_to_all(values, axes, split_axis=0, concat_axis=0, tiled=True)  154 us
    all_to_all x1, waiting for transfers between devices, swap(): return lax.all_to_all(values, axes, split_axis=0, concat_axis=0, tiled=True)  9.11 us
    pallas_call x10, Pallas kernels, run(): pl.pallas_call(body, out_shape=[jax.ShapeDtypeStruct(s, F32) for s in out...  6.53 us
    all_to_all x1, starting transfers between devices, swap(): return lax.all_to_all(values, axes, split_axis=0, concat_axis=0, tiled=True)  6.32 us
  transfers between devices with their start and end apart: 1, of which 1 were waited for; matrix products, arithmetic and copies ran while one was open for 0% of the time, Pallas kernels for 1%

profile of v2, /device:TPU:1, one launch (start us, length us, event | category | flops | bytes accessed | tf_op | source)
XLA Modules:
  0.0 179.5 jit_solution(16180687288903281833)
XLA Ops:
  0.6 2.5 %shard_map.101 = (f32[128,1,256]{2,1,0:T(1,128)}, f32[512,128]{1,0:T(8,128)}, f32[128,128]{1,0:T(8,128)}, f32[128,128]{1,0:T(8,128)}) custom-call(f32[8,16,128]{2,1,0:T(8,128)} %pair_ref.1, s32[8,16]{1,0:T(8,128)} %mask_ref.1, f32[128,512]{1,0:T(8,128)} %win_ref.1, f32[128,128]{1,0:T(8,128)} %wgate_ref.1), custom_call_target="tpu_custom_call" | custom-call | tf_op jit(solution)/shard_map/pallas_call | solution.py:224
  3.2 38.6 %all_to_all.45.msg_ref = f32[128,1,256]{2,1,0:T(1,128)S(1)} all-to-all(f32[128,1,256]{2,1,0:T(1,128)} %get-tuple-element.21), channel_id=1, replica_groups=mesh['x'=4,'zl'=8,'y'=4,'zh'=2,'co'=2] {'co','x','zl','zh'}, dimensions={0} | all-to-all | bytes 262144 | tf_op jit(solution)/shard_map/all_to_all | solution.py:218
  41.7 0.7 shard_map.102
  42.5 11.8 %all_to_all.46.part_ref = f32[8,32,256]{2,1,0:T(8,128)S(1)} all-to-all(f32[8,32,256]{2,1,0:T(8,128)S(1)} %get-tuple-element.22), channel_id=1, replica_groups=mesh['x'=4,'zl'=8,'y'=4,'zh'=2,'co'=2] {'y','co'}, dimensions={0} | all-to-all | bytes 524288 | tf_op jit(solution)/shard_map/all_to_all | solution.py:218
  54.2 0.0 copy-start.4
  54.2 0.3 shard_map.103
  54.6 0.0 copy-start.1
  54.6 0.0 copy-start.3
  54.6 18.0 %all_to_all.47.tri_ref = f32[64,1,256]{2,1,0:T(1,128)S(1)} all-to-all(f32[64,1,256]{2,1,0:T(1,128)S(1)} %shard_map.103), channel_id=1, replica_groups=mesh['x'=4,'zl'=8,'y'=4,'zh'=2,'co'=2] {'x','zl','zh'}, dimensions={0} | all-to-all | bytes 131072 | tf_op jit(solution)/shard_map/all_to_all | solution.py:218
  72.6 0.0 copy-done.4
  72.6 0.0 copy-done.1
  72.6 0.0 copy-done.3
  72.6 0.3 shard_map.104
  72.9 17.9 %all_to_all.48.msg_ref = f32[64,1,256]{2,1,0:T(1,128)S(1)} all-to-all(f32[64,1,256]{2,1,0:T(1,128)S(1)} %shard_map.104), channel_id=1, replica_groups=mesh['x'=4,'zl'=8,'y'=4,'zh'=2,'co'=2] {'x','zl','zh'}, dimensions={0} | all-to-all | bytes 131072 | tf_op jit(solution)/shard_map/all_to_all | solution.py:218
  90.8 0.3 shard_map.105
  91.1 12.3 %all_to_all.49.dtri_ref = f32[8,32,256]{2,1,0:T(8,128)S(1)} all-to-all(f32[8,32,256]{2,1,0:T(8,128)S(1)} %shard_map.105), channel_id=1, replica_groups=mesh['x'=4,'zl'=8,'y'=4,'zh'=2,'co'=2] {'y','co'}, dimensions={0} | all-to-all | bytes 524288 | tf_op jit(solution)/shard_map/all_to_all | solution.py:218
  103.4 0.0 copy-start.7
  103.4 0.0 copy-start.8
  103.4 0.9 shard_map.106
  104.3 0.0 copy-start.2
  104.3 24.0 %all_to_all.50.msg_ref = f32[128,1,256]{2,1,0:T(1,128)S(1)} all-to-all(f32[128,1,256]{2,1,0:T(1,128)S(1)} %shard_map.106), channel_id=1, replica_groups=mesh['x'=4,'zl'=8,'y'=4,'zh'=2,'co'=2] {'co','x','zl','zh'}, dimensions={0} | all-to-all | bytes 262144 | tf_op jit(solution)/shard_map/all_to_all | solution.py:218
  128.3 0.0 copy-done.7
  128.3 0.0 copy-done.8
  128.3 0.0 copy-done.2
  128.3 1.1 shard_map.107
  129.5 14.0 %all_to_all.51.a = f32[32,24,128]{2,1,0:T(8,128)S(1)} all-to-all(f32[32,24,128]{2,1,0:T(8,128)S(1)} %bitcast.1), channel_id=1, replica_groups=mesh['x'=4,'zl'=8,'y'=4,'zh'=2,'co'=2] {'x','y','co'}, dimensions={0} | all-to-all | bytes 786432 | tf_op jit(solution)/shard_map/all_to_all | solution.py:218
  143.5 17.7 %all_to_all.52.a = f32[16,24,128]{2,1,0:T(8,128)S(1)} all-to-all(f32[16,24,128]{2,1,0:T(8,128)S(1)} %shard_map.109), channel_id=1, replica_groups=mesh['x'=4,'zl'=8,'y'=4,'zh'=2,'co'=2] {'zl','zh'}, dimensions={0} | all-to-all | bytes 393216 | tf_op jit(solution)/shard_map/all_to_all | solution.py:218
  161.3 0.8 shard_map.110
  162.0 0.0 copy-start
  162.0 0.0 copy-start.5
  162.0 0.0 copy-start.6
  162.0 6.3 %all-to-all-start.8 = ((f32[32,24,128]{2,1,0:T(8,128)}), f32[32,24,128]{2,1,0:T(8,128)S(1)}, u32[]{:S(2)}, u32[]{:S(2)}) async-start(f32[32,24,128]{2,1,0:T(8,128)} %shard_map.110), calls=%async_computation.8 | async-start | bytes 786432 | tf_op jit(solution)/shard_map/all_to_all | solution.py:218
  168.4 0.0 copy-done
  168.4 0.0 copy-done.5
  168.4 0.0 copy-done.6
  168.4 1.2 shard_map.108
  169.6 9.1 %all-to-all-done.8.parts_ref = f32[32,24,128]{2,1,0:T(8,128)S(1)} async-done(((f32[32,24,128]{2,1,0:T(8,128)}), f32[32,24,128]{2,1,0:T(8,128)S(1)}, u32[]{:S(2)}, u32[]{:S(2)}) %all-to-all-start.8) | async-done | bytes 393248 | tf_op jit(solution)/shard_map/all_to_all | solution.py:218
  178.8 0.8 shard_map.111
  (1 shorter events, 0.0 us)
Async XLA Ops:
  54.2 18.3 %copy-start.4 = (f32[128,128]{1,0:T(8,128)S(1)}, f32[128,128]{1,0:T(8,128)}, u32[]{:S(2)}) copy-start(f32[128,128]{1,0:T(8,128)} %wout_ref.3) | copy-start | bytes 196612
  54.6 18.0 %copy-start.1 = (f32[128,128]{1,0:T(8,128)S(1)}, f32[128,128]{1,0:T(8,128)}, u32[]{:S(2)}) copy-start(f32[128,128]{1,0:T(8,128)} %get-tuple-element.23.gate_ref) | copy-start | bytes 196612
  54.6 18.0 %copy-start.3 = (f32[8,16,128]{2,1,0:T(8,128)S(1)}, f32[8,16,128]{2,1,0:T(8,128)}, u32[]{:S(2)}) copy-start(f32[8,16,128]{2,1,0:T(8,128)} %cot_ref.3) | copy-start | bytes 196612
  103.4 24.9 %copy-start.7 = (f32[128,128]{1,0:T(8,128)S(1)}, f32[128,128]{1,0:T(8,128)}, u32[]{:S(2)}) copy-start(f32[128,128]{1,0:T(8,128)} %get-tuple-element.27.normed_ref) | copy-start | bytes 196612
  103.4 24.9 %copy-start.8 = (s32[8,16]{1,0:T(8,128)S(1)}, s32[8,16]{1,0:T(8,128)}, u32[]{:S(2)}) copy-start(s32[8,16]{1,0:T(8,128)} %mask_ref.1) | copy-start | bytes 1540
  104.3 24.0 %copy-start.2 = (f32[512,128]{1,0:T(8,128)S(1)}, f32[512,128]{1,0:T(8,128)}, u32[]{:S(2)}) copy-start(f32[512,128]{1,0:T(8,128)} %get-tuple-element.26.proj_ref) | copy-start | bytes 786436
  162.0 6.3 %copy-start = (f32[128,512]{1,0:T(8,128)S(1)}, f32[128,512]{1,0:T(8,128)}, u32[]{:S(2)}) copy-start(f32[128,512]{1,0:T(8,128)} %win_ref.1) | copy-start | bytes 786436
  162.0 6.3 %copy-start.5 = (f32[8,16,128]{2,1,0:T(8,128)S(1)}, f32[8,16,128]{2,1,0:T(8,128)}, u32[]{:S(2)}) copy-start(f32[8,16,128]{2,1,0:T(8,128)} %pair_ref.1) | copy-start | bytes 196612
  162.0 6.4 %copy-start.6 = (f32[128,128]{1,0:T(8,128)S(1)}, f32[128,128]{1,0:T(8,128)}, u32[]{:S(2)}) copy-start(f32[128,128]{1,0:T(8,128)} %wgate_ref.1) | copy-start | bytes 196612
  162.0 16.7 %all-to-all-start.8 = ((f32[32,24,128]{2,1,0:T(8,128)}), f32[32,24,128]{2,1,0:T(8,128)S(1)}, u32[]{:S(2)}, u32[]{:S(2)}) async-start(f32[32,24,128]{2,1,0:T(8,128)} %shard_map.110), calls=%async_computation.8 | async-start | bytes 786432 | tf_op jit(solution)/shard_map/all_to_all | solution.py:218

commit v3 on v2

v3 whole, which is shorter than its diff:
```python
import jax
import jax.numpy as jnp
from jax import lax
from jax.experimental import pallas as pl
from jax.experimental.pallas import tpu as pltpu
from jax.sharding import Mesh, PartitionSpec as P

ROW = ("x", "zl")
CH = ("y", "zh", "co")
CHANNELS = ("co", "x", "zl", "zh")
PLANE = ("x", "y", "co")
DEPTH = ("zl", "zh")
F32 = jnp.float32
EPS = 1e-05


def dot(a, b, ca, cb):
    return lax.dot_general(
        a, b, (((ca,), (cb,)), ((), ())), precision=lax.Precision.HIGHEST, preferred_element_type=F32
    )


def call(body, outs, scratch=()):
    vmem = pl.BlockSpec(memory_space=pltpu.VMEM)

    def run(*args):
        return pl.pallas_call(
            body,
            out_shape=[jax.ShapeDtypeStruct(s, F32) for s in outs],
            in_specs=[vmem] * len(args),
            out_specs=[vmem] * len(outs),
            scratch_shapes=[pltpu.VMEM(s, F32) for s in scratch],
            compiler_params=pltpu.CompilerParams(vmem_limit_bytes=32 * 1024 * 1024),
        )(*args)

    return run


def norm_rows(values):
    center = values - jnp.mean(values, axis=1, keepdims=True)
    spread = jnp.mean(center * center, axis=1, keepdims=True)
    rstd = 1.0 / jnp.sqrt(spread + EPS)
    return center * rstd, rstd


def mask_lanes(mask_ref, lanes_ref):
    maskf = mask_ref[...].astype(F32)
    for ii in range(8):
        lanes_ref[0:1, ii * 16 : (ii + 1) * 16] = maskf[ii : ii + 1, :]
    return lanes_ref[0:1, :]


def enter_kernel(
    pair_hbm, mask_hbm, win_hbm, wgate_hbm, msg_hbm, factor_hbm, normed_hbm, gate_hbm,
    pair_ref, mask_ref, win_ref, wgate_ref, msg_ref, factor_ref, normed_ref, gate_ref, lanes_ref, ins, outs
):
    pairs = ((pair_hbm, pair_ref), (mask_hbm, mask_ref), (win_hbm, win_ref), (wgate_hbm, wgate_ref))
    copies = [pltpu.make_async_copy(source, target, ins.at[i]) for i, (source, target) in enumerate(pairs)]
    pairs = ((msg_ref, msg_hbm), (factor_ref, factor_hbm), (normed_ref, normed_hbm), (gate_ref, gate_hbm))
    results = [pltpu.make_async_copy(source, target, outs.at[i]) for i, (source, target) in enumerate(pairs)]
    for copy in copies:
        copy.start()
    copies[0].wait()
    normed, _ = norm_rows(pair_ref[...].reshape(128, 128))
    normed_ref[...] = normed
    results[2].start()
    copies[1].wait()
    maskf = mask_lanes(mask_ref, lanes_ref)
    copies[2].wait()
    proj = dot(win_ref[...], normed, 0, 1)
    for side in range(2):
        base = side * 256
        value = proj[base + 128 : base + 256]
        sig = jax.nn.sigmoid(proj[base : base + 128])
        masked = maskf * sig
        msg_ref[:, 0, side * 128 : (side + 1) * 128] = masked * value
        factor_ref[base : base + 128] = masked
        factor_ref[base + 128 : base + 256] = value * (1.0 - sig)
    results[0].start()
    results[1].start()
    copies[3].wait()
    gate_ref[...] = jax.nn.sigmoid(dot(normed, wgate_ref[...], 1, 0))
    results[3].start()
    for result in results:
        result.wait()


def column_blocks():
    return [
        (y * 64 + co * 32 + zh * 16, y * 64 + zh * 32 + co * 16) for y in range(4) for co in range(2) for zh in range(2)
    ]


def triangle_kernel(msg_ref, part_ref, left_ref, right_ref, flat_ref, turn_ref, natural_ref):
    flat_ref[0] = msg_ref[:, 0, 0:128]
    flat_ref[1] = msg_ref[:, 0, 128:256]
    for co in range(2):
        for zh in range(2):
            source, lanes = pl.ds(co * 64 + zh, 32, stride=2), slice(zh * 32 + co * 16, zh * 32 + co * 16 + 16)
            left, right = flat_ref[0, source, :], flat_ref[1, source, :]
            for s in range(8):
                for x in range(4):
                    rows = slice(x * 64 + s * 8, x * 64 + s * 8 + 8)
                    left_ref[rows, lanes] = left[x * 8 : (x + 1) * 8, s * 16 : (s + 1) * 16]
                turn_ref[s * 32 : (s + 1) * 32, lanes] = right[:, s * 16 : (s + 1) * 16]
    for s in range(8):
        natural_ref[pl.ds(s, 32, stride=8), :] = turn_ref[s * 32 : (s + 1) * 32, :]
    for to, at in column_blocks():
        right_ref[to : to + 16, :] = natural_ref[at : at + 16, :]
    part = dot(right_ref[...], left_ref[...], 1, 1)
    for x, y, co, zh in plane_blocks():
        row = y * 64 + co * 32 + zh * 16
        part_ref[(x * 4 + y) * 2 + co, :, zh * 64 : (zh + 1) * 64] = part[row : row + 16, x * 64 : (x + 1) * 64]


def plane_blocks():
    return [(x, y, co, zh) for x in range(4) for y in range(4) for co in range(2) for zh in range(2)]


def home_kernel(part_ref, msg_ref, rows_ref):
    for co in range(2):
        for x in range(4):
            at, to = x * 8 + co, (co * 4 + x) * 16
            rows_ref[to : to + 16, :] = (part_ref[at] + part_ref[at + 2]) + (part_ref[at + 4] + part_ref[at + 6])
    rows_ref[...] = rows_ref[...].T
    for zl in range(8):
        for zh in range(2):
            msg_ref[zl * 2 + zh] = rows_ref[pl.ds(zh * 64 + zl, 8, stride=8), :]


def norm_channels(values):
    center = values - jnp.mean(values, axis=0, keepdims=True)
    spread = jnp.mean(center * center, axis=0, keepdims=True)
    rstd = 1.0 / jnp.sqrt(spread + EPS)
    return center * rstd, rstd


def turn_kernel(home_ref, cot_ref, gate_ref, wout_ref, msg_ref, tri_ref, flat_ref, turn_ref):
    flat_ref[...] = home_ref[...].reshape(128, 128)
    for s in range(8):
        block = flat_ref[pl.ds(s, 16, stride=8), :]
        for a in range(8):
            tri_ref[a * 16 : (a + 1) * 16, s * 16 : (s + 1) * 16] = block[:, a * 16 : (a + 1) * 16]
    normed, rstd = norm_channels(tri_ref[...])
    d_out = cot_ref[...].reshape(128, 128) * gate_ref[...]
    d_normed = dot(wout_ref[...], d_out, 1, 1)
    along = jnp.mean(d_normed * normed, axis=0, keepdims=True)
    d_tri = rstd * (d_normed - jnp.mean(d_normed, axis=0, keepdims=True) - normed * along)
    for s in range(8):
        for a in range(8):
            turn_ref[s, :, a * 16 : (a + 1) * 16] = d_tri[a * 16 : (a + 1) * 16, s * 16 : (s + 1) * 16]
        flat_ref[pl.ds(s, 16, stride=8), :] = turn_ref[s]
    msg_ref[...] = flat_ref[...].reshape(16, 8, 128)


def spread_kernel(msg_ref, out_ref, flat_ref, rows_ref):
    flat_ref[...] = msg_ref[...].reshape(128, 128)
    for zh in range(2):
        for s in range(8):
            to = zh * 64 + s * 8
            rows_ref[to : to + 8, :] = flat_ref[pl.ds(zh * 8 + s, 8, stride=16), :]
    turned = rows_ref[...].T
    for x in range(4):
        for co in range(2):
            block = turned[(co * 4 + x) * 16 : (co * 4 + x) * 16 + 16]
            for y in range(4):
                out_ref[(x * 4 + y) * 2 + co] = block


def back_kernel(
    dtri_ref, left_ref, right_ref, msg_ref, whole_ref, flat_ref, blocks_ref, natural_ref, turn_ref
):
    for x, y, co, zh in plane_blocks():
        row = y * 64 + co * 32 + zh * 16
        whole_ref[row : row + 16, x * 64 : (x + 1) * 64] = dtri_ref[
            (x * 4 + y) * 2 + co, :, zh * 64 : (zh + 1) * 64
        ]
    dtri = whole_ref[...]
    blocks_ref[...] = dot(dtri, left_ref[...], 1, 0)
    d_left = dot(dtri, right_ref[...], 0, 0)
    for at, to in column_blocks():
        natural_ref[to : to + 16, :] = blocks_ref[at : at + 16, :]
    for s in range(8):
        d_right = natural_ref[pl.ds(s, 32, stride=8), :]
        to = slice(s * 16, (s + 1) * 16)
        for co in range(2):
            for zh in range(2):
                lanes = slice(zh * 32 + co * 16, zh * 32 + co * 16 + 16)
                for x in range(4):
                    row = x * 64 + s * 8
                    turn_ref[0, co, zh, x * 8 : (x + 1) * 8, to] = d_left[row : row + 8, lanes]
                turn_ref[1, co, zh, :, to] = d_right[:, lanes]
    for side in range(2):
        for co in range(2):
            for zh in range(2):
                flat_ref[side, pl.ds(co * 64 + zh, 32, stride=2), :] = turn_ref[side, co, zh]
        msg_ref[:, 0, side * 128 : (side + 1) * 128] = flat_ref[side]


def weights_kernel(
    msg_ref, factor_ref, normed_ref, tri_ref, cot_ref, gate_ref, wout_ref, weights_ref, dproj_ref, dpre_ref, out_ref
):
    normed = normed_ref[...]
    normed_tri, _ = norm_channels(tri_ref[...])
    gate = gate_ref[...]
    cot = cot_ref[...].reshape(128, 128)
    out_proj = dot(normed_tri, wout_ref[...], 0, 0)
    out_ref[...] = out_proj
    d_pre = cot * out_proj * gate * (1.0 - gate)
    dpre_ref[...] = d_pre
    weights_ref[512:640] = dot(normed, d_pre, 0, 0)
    weights_ref[640:768] = dot(normed_tri, cot * gate, 1, 0)
    for side in range(2):
        base = side * 256
        d_value = msg_ref[:, 0, side * 128 : (side + 1) * 128] * factor_ref[base : base + 128]
        d_gate = d_value * factor_ref[base + 128 : base + 256]
        dproj_ref[base : base + 128] = d_gate
        dproj_ref[base + 128 : base + 256] = d_value
        weights_ref[base : base + 128] = dot(normed, d_gate, 0, 1)
        weights_ref[base + 128 : base + 256] = dot(normed, d_value, 0, 1)


def leave_kernel(dproj_ref, dpre_ref, out_ref, gate_ref, pair_ref, win_ref, wgate_ref, dpair_ref, upd_ref):
    upd_ref[...] = (gate_ref[...] * out_ref[...]).reshape(8, 16, 128)
    normed, rstd = norm_rows(pair_ref[...].reshape(128, 128))
    d_normed = dot(dproj_ref[...], win_ref[...], 0, 1) + dot(dpre_ref[...], wgate_ref[...], 1, 1)
    along = jnp.mean(d_normed * normed, axis=1, keepdims=True)
    d_pair = rstd * (d_normed - jnp.mean(d_normed, axis=1, keepdims=True) - normed * along)
    dpair_ref[...] = d_pair.reshape(8, 16, 128)


def sum_kernel(scale, parts_ref, out_ref):
    total = jnp.sum(parts_ref[...], axis=0) * scale
    for i in range(out_ref.shape[0]):
        out_ref[i] = total


def unpack_kernel(parts_ref, dwin_ref, dwg_ref, dwo_ref):
    whole = parts_ref[...].reshape(768, 128)
    for f in range(4):
        dwin_ref[:, f * 128 : (f + 1) * 128] = whole[f * 128 : (f + 1) * 128]
    dwg_ref[...] = whole[512:640]
    dwo_ref[...] = whole[640:768]


def swap(values, axes):
    return lax.all_to_all(values, axes, split_axis=0, concat_axis=0, tiled=True)


def enter(pair, pair_mask, w_in, w_gate):
    held = [(128, 1, 256), (512, 128), (128, 128), (128, 128)]
    return pl.pallas_call(
        enter_kernel,
        out_shape=[jax.ShapeDtypeStruct(s, F32) for s in held],
        in_specs=[pl.BlockSpec(memory_space=pl.ANY)] * 4,
        out_specs=[pl.BlockSpec(memory_space=pl.ANY)] * 4,
        scratch_shapes=[
            pltpu.VMEM(pair.shape, F32),
            pltpu.VMEM(pair_mask.shape, pair_mask.dtype),
            pltpu.VMEM(w_in.shape, F32),
            pltpu.VMEM(w_gate.shape, F32),
            *[pltpu.VMEM(s, F32) for s in held],
            pltpu.VMEM((8, 128), F32),
            pltpu.SemaphoreType.DMA((4,)),
            pltpu.SemaphoreType.DMA((4,)),
        ],
        compiler_params=pltpu.CompilerParams(vmem_limit_bytes=60 * 1024 * 1024),
    )(pair, pair_mask, w_in, w_gate)


def shards(pair, pair_mask, w_in, w_gate, w_out, cotangent):
    msg, factor, normed, gate = enter(pair, pair_mask, w_in, w_gate)
    msg = swap(msg, CHANNELS)
    part, left, right = call(
        triangle_kernel,
        [(32, 16, 128), (256, 64), (256, 64)],
        [(2, 128, 128), (256, 64), (256, 64)],
    )(msg)
    part = swap(part, PLANE)
    (msg,) = call(home_kernel, [(16, 8, 128)], [(128, 128)])(part)
    msg = swap(msg, DEPTH)
    msg, tri = call(turn_kernel, [(16, 8, 128), (128, 128)], [(128, 128), (8, 16, 128)])(
        msg, cotangent, gate, w_out
    )
    msg = swap(msg, DEPTH)
    (d_tri,) = call(spread_kernel, [(32, 16, 128)], [(128, 128), (128, 128)])(msg)
    d_tri = swap(d_tri, PLANE)
    (msg,) = call(
        back_kernel,
        [(128, 1, 256)],
        [(256, 256), (2, 128, 128), (256, 64), (256, 64), (2, 2, 2, 32, 128)],
    )(d_tri, left, right)
    msg = swap(msg, CHANNELS)
    weights, d_proj, d_pre, out_proj = call(
        weights_kernel, [(768, 128), (512, 128), (128, 128), (128, 128)]
    )(msg, factor, normed, tri, cotangent, gate, w_out)
    parts = swap(weights.reshape(32, 24, 128), PLANE)
    d_pair, update = call(leave_kernel, [(8, 16, 128), (8, 16, 128)])(
        d_proj, d_pre, out_proj, gate, pair, w_in, w_gate
    )
    (parts,) = call(lambda a, b: sum_kernel(1.0, a, b), [(16, 24, 128)])(parts)
    parts = swap(parts, DEPTH)
    scale = 1.0 / (pair.shape[0] * lax.axis_size(ROW))
    (parts,) = call(lambda a, b: sum_kernel(scale, a, b), [(32, 24, 128)])(parts)
    parts = swap(parts, PLANE)
    d_win, d_wgate, d_wout = call(unpack_kernel, [(128, 512), (128, 128), (128, 128)])(parts)
    return (update, d_pair, d_win, d_wgate, d_wout)


def solution(mesh):
    fine = Mesh(mesh.devices.reshape(4, 8, 4, 2, 2), ("x", "zl", "y", "zh", "co"))
    in_specs = (P(ROW, CH, None), P(ROW, CH), P(), P(), P(), P(ROW, CH, None))
    out_specs = (P(ROW, CH, None), P(ROW, CH, None), P(), P(), P())
    return jax.shard_map(shards, mesh=fine, in_specs=in_specs, out_specs=out_specs, check_vma=False)
```

time: 180 us -> 179 us (level)
  blocking collectives: 154 us -> 152 us
    all_to_all x8, blocking collectives: 154 us -> 152 us  [swap(): return lax.all_to_all(values, axes, split_axis=0, concat_axis=0, tiled=True)]
where the time goes in v3:
time: 179 us; the launch traced here: 178 us
  blocking collectives  152 us (85%)
  waiting for transfers between devices  9.07 us (5%)
  Pallas kernels  8.99 us (5%)
  starting transfers between devices  6.49 us (4%)
    all_to_all x8, blocking collectives, swap(): return lax.all_to_all(values, axes, split_axis=0, concat_axis=0, tiled=True)  152 us
    all_to_all x1, waiting for transfers between devices, swap(): return lax.all_to_all(values, axes, split_axis=0, concat_axis=0, tiled=True)  9.07 us
    all_to_all x1, starting transfers between devices, swap(): return lax.all_to_all(values, axes, split_axis=0, concat_axis=0, tiled=True)  6.49 us
    pallas_call x10, Pallas kernels, run(): pl.pallas_call(body, out_shape=[jax.ShapeDtypeStruct(s, F32) for s in out...  6.43 us
  transfers between devices with their start and end apart: 1, of which 1 were waited for; matrix products, arithmetic and copies ran while one was open for 0% of the time, Pallas kernels for 1%

profile of v3, /device:TPU:1, one launch (start us, length us, event | category | flops | bytes accessed | tf_op | source)
XLA Modules:
  0.0 177.6 jit_solution(10064436330560491730)
XLA Ops:
  0.6 2.6 %shard_map.101 = (f32[128,1,256]{2,1,0:T(1,128)}, f32[512,128]{1,0:T(8,128)}, f32[128,128]{1,0:T(8,128)}, f32[128,128]{1,0:T(8,128)}) custom-call(f32[8,16,128]{2,1,0:T(8,128)} %pair_ref.1, s32[8,16]{1,0:T(8,128)} %mask_hbm.1, f32[128,512]{1,0:T(8,128)} %win_ref.1, f32[128,128]{1,0:T(8,128)} %wgate_ref.1), custom_call_target="tpu_custom_call" | custom-call | tf_op jit(solution)/shard_map/pallas_call | solution.py:252
  3.2 38.6 %all_to_all.45.msg_ref = f32[128,1,256]{2,1,0:T(1,128)S(1)} all-to-all(f32[128,1,256]{2,1,0:T(1,128)} %get-tuple-element.23), channel_id=1, replica_groups=mesh['x'=4,'zl'=8,'y'=4,'zh'=2,'co'=2] {'co','x','zl','zh'}, dimensions={0} | all-to-all | bytes 262144 | tf_op jit(solution)/shard_map/all_to_all | solution.py:247
  41.8 0.8 shard_map.102
  42.6 14.4 %all_to_all.46.part_ref = f32[32,16,128]{2,1,0:T(8,128)S(1)} all-to-all(f32[32,16,128]{2,1,0:T(8,128)S(1)} %get-tuple-element.24), channel_id=1, replica_groups=mesh['x'=4,'zl'=8,'y'=4,'zh'=2,'co'=2] {'x','y','co'}, dimensions={0} | all-to-all | bytes 524288 | tf_op jit(solution)/shard_map/all_to_all | solution.py:247
  57.0 0.0 copy-start.6
  57.0 0.1 shard_map.103
  57.1 0.0 copy-start.1
  57.1 0.0 copy-start.5
  57.1 14.9 %all_to_all.47.home_ref = f32[16,8,128]{2,1,0:T(8,128)S(1)} all-to-all(f32[16,8,128]{2,1,0:T(8,128)S(1)} %shard_map.103), channel_id=1, replica_groups=mesh['x'=4,'zl'=8,'y'=4,'zh'=2,'co'=2] {'zl','zh'}, dimensions={0} | all-to-all | bytes 131072 | tf_op jit(solution)/shard_map/all_to_all | solution.py:247
  72.0 0.0 copy-done.6
  72.0 0.0 copy-done.1
  72.0 0.0 copy-done.5
  72.0 0.5 shard_map.104
  72.6 15.3 %all_to_all.48.msg_ref = f32[16,8,128]{2,1,0:T(8,128)S(1)} all-to-all(f32[16,8,128]{2,1,0:T(8,128)S(1)} %get-tuple-element.26), channel_id=1, replica_groups=mesh['x'=4,'zl'=8,'y'=4,'zh'=2,'co'=2] {'zl','zh'}, dimensions={0} | all-to-all | bytes 131072 | tf_op jit(solution)/shard_map/all_to_all | solution.py:247
  87.9 0.1 shard_map.105
  88.0 14.3 %all_to_all.49.dtri_ref = f32[32,16,128]{2,1,0:T(8,128)S(1)} all-to-all(f32[32,16,128]{2,1,0:T(8,128)S(1)} %shard_map.105), channel_id=1, replica_groups=mesh['x'=4,'zl'=8,'y'=4,'zh'=2,'co'=2] {'x','y','co'}, dimensions={0} | all-to-all | bytes 524288 | tf_op jit(solution)/shard_map/all_to_all | solution.py:247
  102.3 0.0 copy-start.7
  102.3 1.0 shard_map.106
  103.3 0.0 copy-start.2
  103.4 23.1 %all_to_all.50.msg_ref = f32[128,1,256]{2,1,0:T(1,128)S(1)} all-to-all(f32[128,1,256]{2,1,0:T(1,128)S(1)} %shard_map.106), channel_id=1, replica_groups=mesh['x'=4,'zl'=8,'y'=4,'zh'=2,'co'=2] {'co','x','zl','zh'}, dimensions={0} | all-to-all | bytes 262144 | tf_op jit(solution)/shard_map/all_to_all | solution.py:247
  126.5 0.0 copy-done.7
  126.5 0.0 copy-done.2
  126.5 1.0 shard_map.107
  127.5 14.0 %all_to_all.51.a = f32[32,24,128]{2,1,0:T(8,128)S(1)} all-to-all(f32[32,24,128]{2,1,0:T(8,128)S(1)} %bitcast.1), channel_id=1, replica_groups=mesh['x'=4,'zl'=8,'y'=4,'zh'=2,'co'=2] {'x','y','co'}, dimensions={0} | all-to-all | bytes 786432 | tf_op jit(solution)/shard_map/all_to_all | solution.py:247
  141.6 17.6 %all_to_all.52.a = f32[16,24,128]{2,1,0:T(8,128)S(1)} all-to-all(f32[16,24,128]{2,1,0:T(8,128)S(1)} %shard_map.109), channel_id=1, replica_groups=mesh['x'=4,'zl'=8,'y'=4,'zh'=2,'co'=2] {'zl','zh'}, dimensions={0} | all-to-all | bytes 393216 | tf_op jit(solution)/shard_map/all_to_all | solution.py:247
  159.2 0.8 shard_map.110
  160.0 0.0 copy-start
  160.0 0.0 copy-start.3
  160.0 0.0 copy-start.4
  160.0 6.5 %all-to-all-start.8 = ((f32[32,24,128]{2,1,0:T(8,128)}), f32[32,24,128]{2,1,0:T(8,128)S(1)}, u32[]{:S(2)}, u32[]{:S(2)}) async-start(f32[32,24,128]{2,1,0:T(8,128)} %shard_map.110), calls=%async_computation.8 | async-start | bytes 786432 | tf_op jit(solution)/shard_map/all_to_all | solution.py:247
  166.5 0.0 copy-done
  166.5 0.0 copy-done.3
  166.5 0.0 copy-done.4
  166.5 1.2 shard_map.108
  167.8 9.1 %all-to-all-done.8.parts_ref = f32[32,24,128]{2,1,0:T(8,128)S(1)} async-done(((f32[32,24,128]{2,1,0:T(8,128)}), f32[32,24,128]{2,1,0:T(8,128)S(1)}, u32[]{:S(2)}, u32[]{:S(2)}) %all-to-all-start.8) | async-done | bytes 393248 | tf_op jit(solution)/shard_map/all_to_all | solution.py:247
  176.8 0.8 shard_map.111
  (1 shorter events, 0.0 us)
Async XLA Ops:
  57.0 15.0 %copy-start.6 = (f32[128,128]{1,0:T(8,128)S(1)}, f32[128,128]{1,0:T(8,128)}, u32[]{:S(2)}) copy-start(f32[128,128]{1,0:T(8,128)} %wout_ref.3) | copy-start | bytes 196612
  57.1 14.9 %copy-start.1 = (f32[128,128]{1,0:T(8,128)S(1)}, f32[128,128]{1,0:T(8,128)}, u32[]{:S(2)}) copy-start(f32[128,128]{1,0:T(8,128)} %get-tuple-element.25.gate_ref) | copy-start | bytes 196612
  57.1 14.9 %copy-start.5 = (f32[8,16,128]{2,1,0:T(8,128)S(1)}, f32[8,16,128]{2,1,0:T(8,128)}, u32[]{:S(2)}) copy-start(f32[8,16,128]{2,1,0:T(8,128)} %cot_ref.3) | copy-start | bytes 196612
  102.3 24.2 %copy-start.7 = (f32[128,128]{1,0:T(8,128)S(1)}, f32[128,128]{1,0:T(8,128)}, u32[]{:S(2)}) copy-start(f32[128,128]{1,0:T(8,128)} %get-tuple-element.30.normed_ref) | copy-start | bytes 196612
  103.3 23.1 %copy-start.2 = (f32[512,128]{1,0:T(8,128)S(1)}, f32[512,128]{1,0:T(8,128)}, u32[]{:S(2)}) copy-start(f32[512,128]{1,0:T(8,128)} %get-tuple-element.29.factor_ref) | copy-start | bytes 786436
  160.0 6.5 %copy-start = (f32[128,512]{1,0:T(8,128)S(1)}, f32[128,512]{1,0:T(8,128)}, u32[]{:S(2)}) copy-start(f32[128,512]{1,0:T(8,128)} %win_ref.1) | copy-start | bytes 786436
  160.0 6.5 %copy-start.3 = (f32[8,16,128]{2,1,0:T(8,128)S(1)}, f32[8,16,128]{2,1,0:T(8,128)}, u32[]{:S(2)}) copy-start(f32[8,16,128]{2,1,0:T(8,128)} %pair_ref.1) | copy-start | bytes 196612
  160.0 6.5 %copy-start.4 = (f32[128,128]{1,0:T(8,128)S(1)}, f32[128,128]{1,0:T(8,128)}, u32[]{:S(2)}) copy-start(f32[128,128]{1,0:T(8,128)} %wgate_ref.1) | copy-start | bytes 196612
  160.0 16.8 %all-to-all-start.8 = ((f32[32,24,128]{2,1,0:T(8,128)}), f32[32,24,128]{2,1,0:T(8,128)S(1)}, u32[]{:S(2)}, u32[]{:S(2)}) async-start(f32[32,24,128]{2,1,0:T(8,128)} %shard_map.110), calls=%async_computation.8 | async-start | bytes 786432 | tf_op jit(solution)/shard_map/all_to_all | solution.py:247

commit v4 on v3

--- a/solution.py
+++ b/solution.py
@@ -177,7 +177,7 @@
         ]
     dtri = whole_ref[...]
     blocks_ref[...] = dot(dtri, left_ref[...], 1, 0)
-    d_left = dot(dtri, right_ref[...], 0, 0)
+    d_left = dot(right_ref[...], dtri, 0, 0).T
     for at, to in column_blocks():
         natural_ref[to : to + 16, :] = blocks_ref[at : at + 16, :]
     for s in range(8):
@@ -216,31 +216,31 @@
         d_gate = d_value * factor_ref[base + 128 : base + 256]
         dproj_ref[base : base + 128] = d_gate
         dproj_ref[base + 128 : base + 256] = d_value
-        weights_ref[base : base + 128] = dot(normed, d_gate, 0, 1)
-        weights_ref[base + 128 : base + 256] = dot(normed, d_value, 0, 1)
-
-
-def leave_kernel(dproj_ref, dpre_ref, out_ref, gate_ref, pair_ref, win_ref, wgate_ref, dpair_ref, upd_ref):
+    d_win = dot(normed, dproj_ref[...], 0, 1)
+    for f in range(4):
+        weights_ref[f * 128 : (f + 1) * 128] = d_win[:, f * 128 : (f + 1) * 128]
+
+
+def sum_kernel(scale, parts_ref, out_ref):
+    total = jnp.sum(parts_ref[...], axis=0) * scale
+    for i in range(out_ref.shape[0]):
+        out_ref[i] = total
+
+
+def leave_kernel(
+    parts_ref, dproj_ref, dpre_ref, out_ref, gate_ref, pair_ref, win_ref, wgate_ref,
+    dpair_ref, upd_ref, dwin_ref, dwg_ref, dwo_ref
+):
+    for f in range(4):
+        dwin_ref[:, f * 128 : (f + 1) * 128] = parts_ref[...].reshape(768, 128)[f * 128 : (f + 1) * 128]
+    dwg_ref[...] = parts_ref[...].reshape(768, 128)[512:640]
+    dwo_ref[...] = parts_ref[...].reshape(768, 128)[640:768]
     upd_ref[...] = (gate_ref[...] * out_ref[...]).reshape(8, 16, 128)
     normed, rstd = norm_rows(pair_ref[...].reshape(128, 128))
     d_normed = dot(dproj_ref[...], win_ref[...], 0, 1) + dot(dpre_ref[...], wgate_ref[...], 1, 1)
     along = jnp.mean(d_normed * normed, axis=1, keepdims=True)
     d_pair = rstd * (d_normed - jnp.mean(d_normed, axis=1, keepdims=True) - normed * along)
     dpair_ref[...] = d_pair.reshape(8, 16, 128)
-
-
-def sum_kernel(scale, parts_ref, out_ref):
-    total = jnp.sum(parts_ref[...], axis=0) * scale
-    for i in range(out_ref.shape[0]):
-        out_ref[i] = total
-
-
-def unpack_kernel(parts_ref, dwin_ref, dwg_ref, dwo_ref):
-    whole = parts_ref[...].reshape(768, 128)
-    for f in range(4):
-        dwin_ref[:, f * 128 : (f + 1) * 128] = whole[f * 128 : (f + 1) * 128]
-    dwg_ref[...] = whole[512:640]
-    dwo_ref[...] = whole[640:768]
 
 
 def swap(values, axes):
@@ -295,15 +295,14 @@
         weights_kernel, [(768, 128), (512, 128), (128, 128), (128, 128)]
     )(msg, factor, normed, tri, cotangent, gate, w_out)
     parts = swap(weights.reshape(32, 24, 128), PLANE)
-    d_pair, update = call(leave_kernel, [(8, 16, 128), (8, 16, 128)])(
-        d_proj, d_pre, out_proj, gate, pair, w_in, w_gate
-    )
     (parts,) = call(lambda a, b: sum_kernel(1.0, a, b), [(16, 24, 128)])(parts)
     parts = swap(parts, DEPTH)
     scale = 1.0 / (pair.shape[0] * lax.axis_size(ROW))
     (parts,) = call(lambda a, b: sum_kernel(scale, a, b), [(32, 24, 128)])(parts)
     parts = swap(parts, PLANE)
-    d_win, d_wgate, d_wout = call(unpack_kernel, [(128, 512), (128, 128), (128, 128)])(parts)
+    d_pair, update, d_win, d_wgate, d_wout = call(
+        leave_kernel, [(8, 16, 128), (8, 16, 128), (128, 512), (128, 128), (128, 128)]
+    )(parts, d_proj, d_pre, out_proj, gate, pair, w_in, w_gate)
     return (update, d_pair, d_win, d_wgate, d_wout)
 
 

time: 179 us -> 178 us (level)
  blocking collectives: 152 us -> 169 us
  waiting for transfers between devices: 9.07 us -> 0 us
  starting transfers between devices: 6.49 us -> 0 us
    all_to_all x8 -> x9, blocking collectives: 152 us -> 169 us  [swap(): return lax.all_to_all(values, axes, split_axis=0, concat_axis=0, tiled=True)]
    all_to_all x1 -> x0, waiting for transfers between devices: 9.07 us -> none  [swap(): return lax.all_to_all(values, axes, split_axis=0, concat_axis=0, tiled=True)]
    all_to_all x1 -> x0, starting transfers between devices: 6.49 us -> none  [swap(): return lax.all_to_all(values, axes, split_axis=0, concat_axis=0, tiled=True)]
    pallas_call x10 -> x9, Pallas kernels: 6.43 us -> 4.79 us  [run(): pl.pallas_call(body, out_shape=[jax.ShapeDtypeStruct(s, F32) for s in out...]
  transfers between devices with their start and end apart: 1 -> 0, of which waited for: 1 -> 0; matrix products, arithmetic and copies ran while one was open for 0% -> 0% of each run, Pallas kernels for 1% -> 0%
where the time goes in v4:
time: 178 us; the launch traced here: 177 us
  blocking collectives  169 us (95%)
  Pallas kernels  7.35 us (4%)
    all_to_all x9, blocking collectives, swap(): return lax.all_to_all(values, axes, split_axis=0, concat_axis=0, tiled=True)  169 us
    pallas_call x9, Pallas kernels, run(): pl.pallas_call(body, out_shape=[jax.ShapeDtypeStruct(s, F32) for s in out...  4.79 us

profile of v4, /device:TPU:1, one launch (start us, length us, event | category | flops | bytes accessed | tf_op | source)
XLA Modules:
  0.0 177.0 jit_solution(5517777485803077644)
XLA Ops:
  0.6 2.6 %shard_map.101 = (f32[128,1,256]{2,1,0:T(1,128)}, f32[512,128]{1,0:T(8,128)}, f32[128,128]{1,0:T(8,128)}, f32[128,128]{1,0:T(8,128)}) custom-call(f32[8,16,128]{2,1,0:T(8,128)} %pair_ref.1, s32[8,16]{1,0:T(8,128)} %mask_hbm.1, f32[128,512]{1,0:T(8,128)} %win_ref.1, f32[128,128]{1,0:T(8,128)} %wgate_ref.1), custom_call_target="tpu_custom_call" | custom-call | tf_op jit(solution)/shard_map/pallas_call | solution.py:252
  3.2 38.6 %all_to_all.45.msg_ref = f32[128,1,256]{2,1,0:T(1,128)S(1)} all-to-all(f32[128,1,256]{2,1,0:T(1,128)} %get-tuple-element.23), channel_id=1, replica_groups=mesh['x'=4,'zl'=8,'y'=4,'zh'=2,'co'=2] {'co','x','zl','zh'}, dimensions={0} | all-to-all | bytes 262144 | tf_op jit(solution)/shard_map/all_to_all | solution.py:247
  41.8 0.8 shard_map.102
  42.6 14.4 %all_to_all.46.part_ref = f32[32,16,128]{2,1,0:T(8,128)S(1)} all-to-all(f32[32,16,128]{2,1,0:T(8,128)S(1)} %get-tuple-element.24), channel_id=1, replica_groups=mesh['x'=4,'zl'=8,'y'=4,'zh'=2,'co'=2] {'x','y','co'}, dimensions={0} | all-to-all | bytes 524288 | tf_op jit(solution)/shard_map/all_to_all | solution.py:247
  57.0 0.0 copy-start.6
  57.0 0.1 shard_map.103
  57.1 0.0 copy-start.1
  57.1 0.0 copy-start.5
  57.1 14.9 %all_to_all.47.home_ref = f32[16,8,128]{2,1,0:T(8,128)S(1)} all-to-all(f32[16,8,128]{2,1,0:T(8,128)S(1)} %shard_map.103), channel_id=1, replica_groups=mesh['x'=4,'zl'=8,'y'=4,'zh'=2,'co'=2] {'zl','zh'}, dimensions={0} | all-to-all | bytes 131072 | tf_op jit(solution)/shard_map/all_to_all | solution.py:247
  72.0 0.0 copy-done.6
  72.0 0.0 copy-done.1
  72.0 0.0 copy-done.5
  72.0 0.5 shard_map.104
  72.6 15.3 %all_to_all.48.msg_ref = f32[16,8,128]{2,1,0:T(8,128)S(1)} all-to-all(f32[16,8,128]{2,1,0:T(8,128)S(1)} %get-tuple-element.26), channel_id=1, replica_groups=mesh['x'=4,'zl'=8,'y'=4,'zh'=2,'co'=2] {'zl','zh'}, dimensions={0} | all-to-all | bytes 131072 | tf_op jit(solution)/shard_map/all_to_all | solution.py:247
  87.9 0.1 shard_map.105
  88.0 14.3 %all_to_all.49.dtri_ref = f32[32,16,128]{2,1,0:T(8,128)S(1)} all-to-all(f32[32,16,128]{2,1,0:T(8,128)S(1)} %shard_map.105), channel_id=1, replica_groups=mesh['x'=4,'zl'=8,'y'=4,'zh'=2,'co'=2] {'x','y','co'}, dimensions={0} | all-to-all | bytes 524288 | tf_op jit(solution)/shard_map/all_to_all | solution.py:247
  102.3 0.0 copy-start.7
  102.3 1.0 shard_map.106
  103.3 0.0 copy-start.4
  103.3 23.1 %all_to_all.50.msg_ref = f32[128,1,256]{2,1,0:T(1,128)S(1)} all-to-all(f32[128,1,256]{2,1,0:T(1,128)S(1)} %shard_map.106), channel_id=1, replica_groups=mesh['x'=4,'zl'=8,'y'=4,'zh'=2,'co'=2] {'co','x','zl','zh'}, dimensions={0} | all-to-all | bytes 262144 | tf_op jit(solution)/shard_map/all_to_all | solution.py:247
  126.5 0.0 copy-done.7
  126.5 0.0 copy-done.4
  126.5 0.9 shard_map.107
  127.3 14.0 %all_to_all.51.a = f32[32,24,128]{2,1,0:T(8,128)S(1)} all-to-all(f32[32,24,128]{2,1,0:T(8,128)S(1)} %bitcast.1), channel_id=1, replica_groups=mesh['x'=4,'zl'=8,'y'=4,'zh'=2,'co'=2] {'x','y','co'}, dimensions={0} | all-to-all | bytes 786432 | tf_op jit(solution)/shard_map/all_to_all | solution.py:247
  141.4 17.6 %all_to_all.52.a = f32[16,24,128]{2,1,0:T(8,128)S(1)} all-to-all(f32[16,24,128]{2,1,0:T(8,128)S(1)} %shard_map.108), channel_id=1, replica_groups=mesh['x'=4,'zl'=8,'y'=4,'zh'=2,'co'=2] {'zl','zh'}, dimensions={0} | all-to-all | bytes 393216 | tf_op jit(solution)/shard_map/all_to_all | solution.py:247
  159.1 0.0 copy-start
  159.1 0.0 copy-start.2
  159.1 0.0 copy-start.3
  159.1 16.6 %all_to_all.53.parts_ref = f32[32,24,128]{2,1,0:T(8,128)S(1)} all-to-all(f32[32,24,128]{2,1,0:T(8,128)S(1)} %shard_map.109), channel_id=1, replica_groups=mesh['x'=4,'zl'=8,'y'=4,'zh'=2,'co'=2] {'x','y','co'}, dimensions={0} | all-to-all | bytes 786432 | tf_op jit(solution)/shard_map/all_to_all | solution.py:247
  175.7 0.0 copy-done
  175.7 0.0 copy-done.2
  175.7 0.0 copy-done.3
  175.7 1.3 shard_map.110
  (2 shorter events, 0.1 us)
Async XLA Ops:
  57.0 15.0 %copy-start.6 = (f32[128,128]{1,0:T(8,128)S(1)}, f32[128,128]{1,0:T(8,128)}, u32[]{:S(2)}) copy-start(f32[128,128]{1,0:T(8,128)} %wout_ref.3) | copy-start | bytes 196612
  57.1 14.9 %copy-start.1 = (f32[128,128]{1,0:T(8,128)S(1)}, f32[128,128]{1,0:T(8,128)}, u32[]{:S(2)}) copy-start(f32[128,128]{1,0:T(8,128)} %get-tuple-element.25.gate_ref) | copy-start | bytes 196612
  57.1 14.9 %copy-start.5 = (f32[8,16,128]{2,1,0:T(8,128)S(1)}, f32[8,16,128]{2,1,0:T(8,128)}, u32[]{:S(2)}) copy-start(f32[8,16,128]{2,1,0:T(8,128)} %cot_ref.3) | copy-start | bytes 196612
  102.3 24.2 %copy-start.7 = (f32[128,128]{1,0:T(8,128)S(1)}, f32[128,128]{1,0:T(8,128)}, u32[]{:S(2)}) copy-start(f32[128,128]{1,0:T(8,128)} %get-tuple-element.30.normed_ref) | copy-start | bytes 196612
  103.3 23.1 %copy-start.4 = (f32[512,128]{1,0:T(8,128)S(1)}, f32[512,128]{1,0:T(8,128)}, u32[]{:S(2)}) copy-start(f32[512,128]{1,0:T(8,128)} %get-tuple-element.29.factor_ref) | copy-start | bytes 786436
  159.1 16.6 %copy-start = (f32[128,512]{1,0:T(8,128)S(1)}, f32[128,512]{1,0:T(8,128)}, u32[]{:S(2)}) copy-start(f32[128,512]{1,0:T(8,128)} %win_ref.1) | copy-start | bytes 786436
  159.1 16.6 %copy-start.2 = (f32[8,16,128]{2,1,0:T(8,128)S(1)}, f32[8,16,128]{2,1,0:T(8,128)}, u32[]{:S(2)}) copy-start(f32[8,16,128]{2,1,0:T(8,128)} %pair_ref.1) | copy-start | bytes 196612
  159.1 16.6 %copy-start.3 = (f32[128,128]{1,0:T(8,128)S(1)}, f32[128,128]{1,0:T(8,128)}, u32[]{:S(2)}) copy-start(f32[128,128]{1,0:T(8,128)} %wgate_ref.1) | copy-start | bytes 196612

commit v5 on v4

--- a/solution.py
+++ b/solution.py
@@ -7,7 +7,7 @@
 
 ROW = ("x", "zl")
 CH = ("y", "zh", "co")
-CHANNELS = ("co", "x", "zl", "zh")
+CHANNELS = ("zl", "zh", "co", "x")
 PLANE = ("x", "y", "co")
 DEPTH = ("zl", "zh")
 F32 = jnp.float32
@@ -92,17 +92,14 @@
 
 
 def triangle_kernel(msg_ref, part_ref, left_ref, right_ref, flat_ref, turn_ref, natural_ref):
-    flat_ref[0] = msg_ref[:, 0, 0:128]
-    flat_ref[1] = msg_ref[:, 0, 128:256]
-    for co in range(2):
-        for zh in range(2):
-            source, lanes = pl.ds(co * 64 + zh, 32, stride=2), slice(zh * 32 + co * 16, zh * 32 + co * 16 + 16)
-            left, right = flat_ref[0, source, :], flat_ref[1, source, :]
-            for s in range(8):
-                for x in range(4):
-                    rows = slice(x * 64 + s * 8, x * 64 + s * 8 + 8)
-                    left_ref[rows, lanes] = left[x * 8 : (x + 1) * 8, s * 16 : (s + 1) * 16]
-                turn_ref[s * 32 : (s + 1) * 32, lanes] = right[:, s * 16 : (s + 1) * 16]
+    flat_ref[0, 0:128] = msg_ref[:, 0, 0:128]
+    flat_ref[1, 0:128] = msg_ref[:, 0, 128:256]
+    for x, co, zh in channel_blocks():
+        source, lanes = pl.ds(zh * 8 + co * 4 + x, 8, stride=16), slice(zh * 32 + co * 16, zh * 32 + co * 16 + 16)
+        left, right = flat_ref[0, source, :], flat_ref[1, source, :]
+        for s in range(8):
+            left_ref[x * 64 + s * 8 : x * 64 + s * 8 + 8, lanes] = left[:, s * 16 : (s + 1) * 16]
+            turn_ref[s * 32 + x * 8 : s * 32 + x * 8 + 8, lanes] = right[:, s * 16 : (s + 1) * 16]
     for s in range(8):
         natural_ref[pl.ds(s, 32, stride=8), :] = turn_ref[s * 32 : (s + 1) * 32, :]
     for to, at in column_blocks():
@@ -113,6 +110,10 @@
         part_ref[(x * 4 + y) * 2 + co, :, zh * 64 : (zh + 1) * 64] = part[row : row + 16, x * 64 : (x + 1) * 64]
 
 
+def channel_blocks():
+    return [(x, co, zh) for x in range(4) for co in range(2) for zh in range(2)]
+
+
 def plane_blocks():
     return [(x, y, co, zh) for x in range(4) for y in range(4) for co in range(2) for zh in range(2)]
 
@@ -122,7 +123,7 @@
         for x in range(4):
             at, to = x * 8 + co, (co * 4 + x) * 16
             rows_ref[to : to + 16, :] = (part_ref[at] + part_ref[at + 2]) + (part_ref[at + 4] + part_ref[at + 6])
-    rows_ref[...] = rows_ref[...].T
+    rows_ref[0:128] = rows_ref[0:128].T
     for zl in range(8):
         for zh in range(2):
             msg_ref[zl * 2 + zh] = rows_ref[pl.ds(zh * 64 + zl, 8, stride=8), :]
@@ -136,25 +137,31 @@
 
 
 def turn_kernel(home_ref, cot_ref, gate_ref, wout_ref, msg_ref, tri_ref, flat_ref, turn_ref):
-    flat_ref[...] = home_ref[...].reshape(128, 128)
+    flat_ref[0:128] = home_ref[...].reshape(128, 128)
     for s in range(8):
         block = flat_ref[pl.ds(s, 16, stride=8), :]
         for a in range(8):
-            tri_ref[a * 16 : (a + 1) * 16, s * 16 : (s + 1) * 16] = block[:, a * 16 : (a + 1) * 16]
-    normed, rstd = norm_channels(tri_ref[...])
+            turn_ref[a, :, s * 16 : (s + 1) * 16] = block[:, a * 16 : (a + 1) * 16]
+    for a in range(8):
+        flat_ref[pl.ds(a, 16, stride=8), :] = turn_ref[a]
+    tri = flat_ref[0:128]
+    tri_ref[...] = tri
+    normed, rstd = norm_channels(tri)
     d_out = cot_ref[...].reshape(128, 128) * gate_ref[...]
     d_normed = dot(wout_ref[...], d_out, 1, 1)
     along = jnp.mean(d_normed * normed, axis=0, keepdims=True)
-    d_tri = rstd * (d_normed - jnp.mean(d_normed, axis=0, keepdims=True) - normed * along)
+    flat_ref[0:128] = rstd * (d_normed - jnp.mean(d_normed, axis=0, keepdims=True) - normed * along)
+    for a in range(8):
+        block = flat_ref[pl.ds(a, 16, stride=8), :]
+        for s in range(8):
+            turn_ref[s, :, a * 16 : (a + 1) * 16] = block[:, s * 16 : (s + 1) * 16]
     for s in range(8):
-        for a in range(8):
-            turn_ref[s, :, a * 16 : (a + 1) * 16] = d_tri[a * 16 : (a + 1) * 16, s * 16 : (s + 1) * 16]
         flat_ref[pl.ds(s, 16, stride=8), :] = turn_ref[s]
-    msg_ref[...] = flat_ref[...].reshape(16, 8, 128)
+    msg_ref[...] = flat_ref[0:128].reshape(16, 8, 128)
 
 
 def spread_kernel(msg_ref, out_ref, flat_ref, rows_ref):
-    flat_ref[...] = msg_ref[...].reshape(128, 128)
+    flat_ref[0:128] = msg_ref[...].reshape(128, 128)
     for zh in range(2):
         for s in range(8):
             to = zh * 64 + s * 8
@@ -183,18 +190,14 @@
     for s in range(8):
         d_right = natural_ref[pl.ds(s, 32, stride=8), :]
         to = slice(s * 16, (s + 1) * 16)
-        for co in range(2):
-            for zh in range(2):
-                lanes = slice(zh * 32 + co * 16, zh * 32 + co * 16 + 16)
-                for x in range(4):
-                    row = x * 64 + s * 8
-                    turn_ref[0, co, zh, x * 8 : (x + 1) * 8, to] = d_left[row : row + 8, lanes]
-                turn_ref[1, co, zh, :, to] = d_right[:, lanes]
+        for x, co, zh in channel_blocks():
+            lanes = slice(zh * 32 + co * 16, zh * 32 + co * 16 + 16)
+            turn_ref[0, co, zh, x, :, to] = d_left[x * 64 + s * 8 : x * 64 + s * 8 + 8, lanes]
+            turn_ref[1, co, zh, x, :, to] = d_right[x * 8 : (x + 1) * 8, lanes]
     for side in range(2):
-        for co in range(2):
-            for zh in range(2):
-                flat_ref[side, pl.ds(co * 64 + zh, 32, stride=2), :] = turn_ref[side, co, zh]
-        msg_ref[:, 0, side * 128 : (side + 1) * 128] = flat_ref[side]
+        for x, co, zh in channel_blocks():
+            flat_ref[side, pl.ds(zh * 8 + co * 4 + x, 8, stride=16), :] = turn_ref[side, co, zh, x]
+        msg_ref[:, 0, side * 128 : (side + 1) * 128] = flat_ref[side, 0:128]
 
 
 def weights_kernel(
@@ -274,21 +277,21 @@
     part, left, right = call(
         triangle_kernel,
         [(32, 16, 128), (256, 64), (256, 64)],
-        [(2, 128, 128), (256, 64), (256, 64)],
+        [(2, 144, 128), (256, 64), (264, 64)],
     )(msg)
     part = swap(part, PLANE)
-    (msg,) = call(home_kernel, [(16, 8, 128)], [(128, 128)])(part)
+    (msg,) = call(home_kernel, [(16, 8, 128)], [(136, 128)])(part)
     msg = swap(msg, DEPTH)
-    msg, tri = call(turn_kernel, [(16, 8, 128), (128, 128)], [(128, 128), (8, 16, 128)])(
+    msg, tri = call(turn_kernel, [(16, 8, 128), (128, 128)], [(136, 128), (8, 16, 128)])(
         msg, cotangent, gate, w_out
     )
     msg = swap(msg, DEPTH)
-    (d_tri,) = call(spread_kernel, [(32, 16, 128)], [(128, 128), (128, 128)])(msg)
+    (d_tri,) = call(spread_kernel, [(32, 16, 128)], [(144, 128), (128, 128)])(msg)
     d_tri = swap(d_tri, PLANE)
     (msg,) = call(
         back_kernel,
         [(128, 1, 256)],
-        [(256, 256), (2, 128, 128), (256, 64), (256, 64), (2, 2, 2, 32, 128)],
+        [(256, 256), (2, 144, 128), (256, 64), (264, 64), (2, 2, 2, 4, 8, 128)],
     )(d_tri, left, right)
     msg = swap(msg, CHANNELS)
     weights, d_proj, d_pre, out_proj = call(

time: 178 us -> 177 us (level)
  no operation moved by 1% of the time
where the time goes in v5:
time: 177 us
  blocking collectives  169 us (95%)
  Pallas kernels  7.58 us (4%)
    all_to_all x9, blocking collectives, swap(): return lax.all_to_all(values, axes, split_axis=0, concat_axis=0, tiled=True)  169 us
    pallas_call x9, Pallas kernels, run(): pl.pallas_call(body, out_shape=[jax.ShapeDtypeStruct(s, F32) for s in out...  5.02 us

profile of v5, /device:TPU:1, one launch (start us, length us, event | category | flops | bytes accessed | tf_op | source)
XLA Modules:
  0.0 176.9 jit_solution(8265081385252756815)
XLA Ops:
  0.6 2.6 %shard_map.101 = (f32[128,1,256]{2,1,0:T(1,128)}, f32[512,128]{1,0:T(8,128)}, f32[128,128]{1,0:T(8,128)}, f32[128,128]{1,0:T(8,128)}) custom-call(f32[8,16,128]{2,1,0:T(8,128)} %pair_ref.1, s32[8,16]{1,0:T(8,128)} %mask_hbm.1, f32[128,512]{1,0:T(8,128)} %win_ref.1, f32[128,128]{1,0:T(8,128)} %wgate_ref.1), custom_call_target="tpu_custom_call" | custom-call | tf_op jit(solution)/shard_map/pallas_call | solution.py:255
  3.2 35.6 %all_to_all.45.msg_ref = f32[128,1,256]{2,1,0:T(1,128)S(1)} all-to-all(f32[128,1,256]{2,1,0:T(1,128)} %get-tuple-element.23), channel_id=1, replica_groups=mesh['x'=4,'zl'=8,'y'=4,'zh'=2,'co'=2] {'zl','zh','co','x'}, dimensions={0} | all-to-all | bytes 262144 | tf_op jit(solution)/shard_map/all_to_all | solution.py:250
  38.8 0.8 shard_map.102
  39.6 15.7 %all_to_all.46.part_ref = f32[32,16,128]{2,1,0:T(8,128)S(1)} all-to-all(f32[32,16,128]{2,1,0:T(8,128)S(1)} %get-tuple-element.24), channel_id=1, replica_groups=mesh['x'=4,'zl'=8,'y'=4,'zh'=2,'co'=2] {'x','y','co'}, dimensions={0} | all-to-all | bytes 524288 | tf_op jit(solution)/shard_map/all_to_all | solution.py:250
  55.3 0.0 copy-start.6
  55.3 0.1 shard_map.103
  55.4 0.0 copy-start.1
  55.4 0.0 copy-start.5
  55.4 16.4 %all_to_all.47.home_ref = f32[16,8,128]{2,1,0:T(8,128)S(1)} all-to-all(f32[16,8,128]{2,1,0:T(8,128)S(1)} %shard_map.103), channel_id=1, replica_groups=mesh['x'=4,'zl'=8,'y'=4,'zh'=2,'co'=2] {'zl','zh'}, dimensions={0} | all-to-all | bytes 131072 | tf_op jit(solution)/shard_map/all_to_all | solution.py:250
  71.8 0.0 copy-done.6
  71.8 0.0 copy-done.1
  71.8 0.0 copy-done.5
  71.8 0.5 shard_map.104
  72.4 15.3 %all_to_all.48.msg_ref = f32[16,8,128]{2,1,0:T(8,128)S(1)} all-to-all(f32[16,8,128]{2,1,0:T(8,128)S(1)} %get-tuple-element.26), channel_id=1, replica_groups=mesh['x'=4,'zl'=8,'y'=4,'zh'=2,'co'=2] {'zl','zh'}, dimensions={0} | all-to-all | bytes 131072 | tf_op jit(solution)/shard_map/all_to_all | solution.py:250
  87.7 0.1 shard_map.105
  87.8 14.3 %all_to_all.49.dtri_ref = f32[32,16,128]{2,1,0:T(8,128)S(1)} all-to-all(f32[32,16,128]{2,1,0:T(8,128)S(1)} %shard_map.105), channel_id=1, replica_groups=mesh['x'=4,'zl'=8,'y'=4,'zh'=2,'co'=2] {'x','y','co'}, dimensions={0} | all-to-all | bytes 524288 | tf_op jit(solution)/shard_map/all_to_all | solution.py:250
  102.1 0.0 copy-start.7
  102.1 1.2 shard_map.106
  103.3 0.0 copy-start.4
  103.4 20.3 %all_to_all.50.msg_ref = f32[128,1,256]{2,1,0:T(1,128)S(1)} all-to-all(f32[128,1,256]{2,1,0:T(1,128)S(1)} %shard_map.106), channel_id=1, replica_groups=mesh['x'=4,'zl'=8,'y'=4,'zh'=2,'co'=2] {'zl','zh','co','x'}, dimensions={0} | all-to-all | bytes 262144 | tf_op jit(solution)/shard_map/all_to_all | solution.py:250
  123.6 0.0 copy-done.7
  123.6 0.0 copy-done.4
  123.6 0.9 shard_map.107
  124.5 15.3 %all_to_all.51.a = f32[32,24,128]{2,1,0:T(8,128)S(1)} all-to-all(f32[32,24,128]{2,1,0:T(8,128)S(1)} %bitcast.1), channel_id=1, replica_groups=mesh['x'=4,'zl'=8,'y'=4,'zh'=2,'co'=2] {'x','y','co'}, dimensions={0} | all-to-all | bytes 786432 | tf_op jit(solution)/shard_map/all_to_all | solution.py:250
  139.9 19.5 %all_to_all.52.a = f32[16,24,128]{2,1,0:T(8,128)S(1)} all-to-all(f32[16,24,128]{2,1,0:T(8,128)S(1)} %shard_map.108), channel_id=1, replica_groups=mesh['x'=4,'zl'=8,'y'=4,'zh'=2,'co'=2] {'zl','zh'}, dimensions={0} | all-to-all | bytes 393216 | tf_op jit(solution)/shard_map/all_to_all | solution.py:250
  159.5 0.0 copy-start
  159.5 0.0 copy-start.2
  159.5 0.0 copy-start.3
  159.5 16.1 %all_to_all.53.parts_ref = f32[32,24,128]{2,1,0:T(8,128)S(1)} all-to-all(f32[32,24,128]{2,1,0:T(8,128)S(1)} %shard_map.109), channel_id=1, replica_groups=mesh['x'=4,'zl'=8,'y'=4,'zh'=2,'co'=2] {'x','y','co'}, dimensions={0} | all-to-all | bytes 786432 | tf_op jit(solution)/shard_map/all_to_all | solution.py:250
  175.6 0.0 copy-done
  175.6 0.0 copy-done.2
  175.6 0.0 copy-done.3
  175.6 1.3 shard_map.110
  (2 shorter events, 0.1 us)
Async XLA Ops:
  55.3 16.6 %copy-start.6 = (f32[128,128]{1,0:T(8,128)S(1)}, f32[128,128]{1,0:T(8,128)}, u32[]{:S(2)}) copy-start(f32[128,128]{1,0:T(8,128)} %wout_ref.3) | copy-start | bytes 196612
  55.4 16.5 %copy-start.1 = (f32[128,128]{1,0:T(8,128)S(1)}, f32[128,128]{1,0:T(8,128)}, u32[]{:S(2)}) copy-start(f32[128,128]{1,0:T(8,128)} %get-tuple-element.25.gate_ref) | copy-start | bytes 196612
  55.4 16.5 %copy-start.5 = (f32[8,16,128]{2,1,0:T(8,128)S(1)}, f32[8,16,128]{2,1,0:T(8,128)}, u32[]{:S(2)}) copy-start(f32[8,16,128]{2,1,0:T(8,128)} %cot_ref.3) | copy-start | bytes 196612
  102.1 21.5 %copy-start.7 = (f32[128,128]{1,0:T(8,128)S(1)}, f32[128,128]{1,0:T(8,128)}, u32[]{:S(2)}) copy-start(f32[128,128]{1,0:T(8,128)} %get-tuple-element.30.normed_ref) | copy-start | bytes 196612
  103.3 20.3 %copy-start.4 = (f32[512,128]{1,0:T(8,128)S(1)}, f32[512,128]{1,0:T(8,128)}, u32[]{:S(2)}) copy-start(f32[512,128]{1,0:T(8,128)} %get-tuple-element.29.factor_ref) | copy-start | bytes 786436
  159.5 16.1 %copy-start = (f32[128,512]{1,0:T(8,128)S(1)}, f32[128,512]{1,0:T(8,128)}, u32[]{:S(2)}) copy-start(f32[128,512]{1,0:T(8,128)} %win_ref.1) | copy-start | bytes 786436
  159.5 16.1 %copy-start.2 = (f32[8,16,128]{2,1,0:T(8,128)S(1)}, f32[8,16,128]{2,1,0:T(8,128)}, u32[]{:S(2)}) copy-start(f32[8,16,128]{2,1,0:T(8,128)} %pair_ref.1) | copy-start | bytes 196612
  159.5 16.1 %copy-start.3 = (f32[128,128]{1,0:T(8,128)S(1)}, f32[128,128]{1,0:T(8,128)}, u32[]{:S(2)}) copy-start(f32[128,128]{1,0:T(8,128)} %wgate_ref.1) | copy-start | bytes 196612

commit v6 on v5

--- a/solution.py
+++ b/solution.py
@@ -7,9 +7,9 @@
 
 ROW = ("x", "zl")
 CH = ("y", "zh", "co")
-CHANNELS = ("zl", "zh", "co", "x")
+CHANNELS = ("zh", "zl", "co", "x")
 PLANE = ("x", "y", "co")
-DEPTH = ("zl", "zh")
+DEPTH = ("zh", "zl")
 F32 = jnp.float32
 EPS = 1e-05
 
@@ -95,7 +95,7 @@
     flat_ref[0, 0:128] = msg_ref[:, 0, 0:128]
     flat_ref[1, 0:128] = msg_ref[:, 0, 128:256]
     for x, co, zh in channel_blocks():
-        source, lanes = pl.ds(zh * 8 + co * 4 + x, 8, stride=16), slice(zh * 32 + co * 16, zh * 32 + co * 16 + 16)
+        source, lanes = pl.ds(zh * 64 + co * 4 + x, 8, stride=8), slice(zh * 32 + co * 16, zh * 32 + co * 16 + 16)
         left, right = flat_ref[0, source, :], flat_ref[1, source, :]
         for s in range(8):
             left_ref[x * 64 + s * 8 : x * 64 + s * 8 + 8, lanes] = left[:, s * 16 : (s + 1) * 16]
@@ -126,7 +126,7 @@
     rows_ref[0:128] = rows_ref[0:128].T
     for zl in range(8):
         for zh in range(2):
-            msg_ref[zl * 2 + zh] = rows_ref[pl.ds(zh * 64 + zl, 8, stride=8), :]
+            msg_ref[zh * 8 + zl] = rows_ref[pl.ds(zh * 64 + zl, 8, stride=8), :]
 
 
 def norm_channels(values):
@@ -165,7 +165,7 @@
     for zh in range(2):
         for s in range(8):
             to = zh * 64 + s * 8
-            rows_ref[to : to + 8, :] = flat_ref[pl.ds(zh * 8 + s, 8, stride=16), :]
+            rows_ref[to : to + 8, :] = flat_ref[pl.ds(zh * 64 + s, 8, stride=8), :]
     turned = rows_ref[...].T
     for x in range(4):
         for co in range(2):
@@ -196,7 +196,7 @@
             turn_ref[1, co, zh, x, :, to] = d_right[x * 8 : (x + 1) * 8, lanes]
     for side in range(2):
         for x, co, zh in channel_blocks():
-            flat_ref[side, pl.ds(zh * 8 + co * 4 + x, 8, stride=16), :] = turn_ref[side, co, zh, x]
+            flat_ref[side, pl.ds(zh * 64 + co * 4 + x, 8, stride=8), :] = turn_ref[side, co, zh, x]
         msg_ref[:, 0, side * 128 : (side + 1) * 128] = flat_ref[side, 0:128]
 
 

time: 177 us -> 176 us (level)
  blocking collectives: 169 us -> 167 us
where the time goes in v6:
time: 176 us; the launch traced here: 175 us
  blocking collectives  167 us (95%)
  Pallas kernels  7.57 us (4%)
    all_to_all x9, blocking collectives, swap(): return lax.all_to_all(values, axes, split_axis=0, concat_axis=0, tiled=True)  167 us
    pallas_call x9, Pallas kernels, run(): pl.pallas_call(body, out_shape=[jax.ShapeDtypeStruct(s, F32) for s in out...  5.01 us

profile of v6, /device:TPU:1, one launch (start us, length us, event | category | flops | bytes accessed | tf_op | source)
XLA Modules:
  0.0 175.2 jit_solution(4637980469285830267)
XLA Ops:
  0.6 2.6 %shard_map.101 = (f32[128,1,256]{2,1,0:T(1,128)}, f32[512,128]{1,0:T(8,128)}, f32[128,128]{1,0:T(8,128)}, f32[128,128]{1,0:T(8,128)}) custom-call(f32[8,16,128]{2,1,0:T(8,128)} %pair_ref.1, s32[8,16]{1,0:T(8,128)} %mask_hbm.1, f32[128,512]{1,0:T(8,128)} %win_ref.1, f32[128,128]{1,0:T(8,128)} %wgate_ref.1), custom_call_target="tpu_custom_call" | custom-call | tf_op jit(solution)/shard_map/pallas_call | solution.py:255
  3.2 38.5 %all_to_all.45.msg_ref = f32[128,1,256]{2,1,0:T(1,128)S(1)} all-to-all(f32[128,1,256]{2,1,0:T(1,128)} %get-tuple-element.23), channel_id=1, replica_groups=mesh['x'=4,'zl'=8,'y'=4,'zh'=2,'co'=2] {'zh','zl','co','x'}, dimensions={0} | all-to-all | bytes 262144 | tf_op jit(solution)/shard_map/all_to_all | solution.py:250
  41.7 0.8 shard_map.102
  42.6 14.7 %all_to_all.46.part_ref = f32[32,16,128]{2,1,0:T(8,128)S(1)} all-to-all(f32[32,16,128]{2,1,0:T(8,128)S(1)} %get-tuple-element.24), channel_id=1, replica_groups=mesh['x'=4,'zl'=8,'y'=4,'zh'=2,'co'=2] {'x','y','co'}, dimensions={0} | all-to-all | bytes 524288 | tf_op jit(solution)/shard_map/all_to_all | solution.py:250
  57.3 0.0 copy-start.6
  57.3 0.1 shard_map.103
  57.4 0.0 copy-start.1
  57.4 0.0 copy-start.5
  57.4 14.4 %all_to_all.47.home_ref = f32[16,8,128]{2,1,0:T(8,128)S(1)} all-to-all(f32[16,8,128]{2,1,0:T(8,128)S(1)} %shard_map.103), channel_id=1, replica_groups=mesh['x'=4,'zl'=8,'y'=4,'zh'=2,'co'=2] {'zh','zl'}, dimensions={0} | all-to-all | bytes 131072 | tf_op jit(solution)/shard_map/all_to_all | solution.py:250
  71.8 0.0 copy-done.6
  71.8 0.0 copy-done.1
  71.8 0.0 copy-done.5
  71.8 0.5 shard_map.104
  72.4 15.3 %all_to_all.48.msg_ref = f32[16,8,128]{2,1,0:T(8,128)S(1)} all-to-all(f32[16,8,128]{2,1,0:T(8,128)S(1)} %get-tuple-element.26), channel_id=1, replica_groups=mesh['x'=4,'zl'=8,'y'=4,'zh'=2,'co'=2] {'zh','zl'}, dimensions={0} | all-to-all | bytes 131072 | tf_op jit(solution)/shard_map/all_to_all | solution.py:250
  87.6 0.1 shard_map.105
  87.7 14.3 %all_to_all.49.dtri_ref = f32[32,16,128]{2,1,0:T(8,128)S(1)} all-to-all(f32[32,16,128]{2,1,0:T(8,128)S(1)} %shard_map.105), channel_id=1, replica_groups=mesh['x'=4,'zl'=8,'y'=4,'zh'=2,'co'=2] {'x','y','co'}, dimensions={0} | all-to-all | bytes 524288 | tf_op jit(solution)/shard_map/all_to_all | solution.py:250
  102.0 0.0 copy-start.7
  102.0 1.2 shard_map.106
  103.2 0.0 copy-start.4
  103.2 23.3 %all_to_all.50.msg_ref = f32[128,1,256]{2,1,0:T(1,128)S(1)} all-to-all(f32[128,1,256]{2,1,0:T(1,128)S(1)} %shard_map.106), channel_id=1, replica_groups=mesh['x'=4,'zl'=8,'y'=4,'zh'=2,'co'=2] {'zh','zl','co','x'}, dimensions={0} | all-to-all | bytes 262144 | tf_op jit(solution)/shard_map/all_to_all | solution.py:250
  126.5 0.0 copy-done.7
  126.5 0.0 copy-done.4
  126.5 0.9 shard_map.107
  127.4 14.1 %all_to_all.51.a = f32[32,24,128]{2,1,0:T(8,128)S(1)} all-to-all(f32[32,24,128]{2,1,0:T(8,128)S(1)} %bitcast.1), channel_id=1, replica_groups=mesh['x'=4,'zl'=8,'y'=4,'zh'=2,'co'=2] {'x','y','co'}, dimensions={0} | all-to-all | bytes 786432 | tf_op jit(solution)/shard_map/all_to_all | solution.py:250
  141.5 16.6 %all_to_all.52.a = f32[16,24,128]{2,1,0:T(8,128)S(1)} all-to-all(f32[16,24,128]{2,1,0:T(8,128)S(1)} %shard_map.108), channel_id=1, replica_groups=mesh['x'=4,'zl'=8,'y'=4,'zh'=2,'co'=2] {'zh','zl'}, dimensions={0} | all-to-all | bytes 393216 | tf_op jit(solution)/shard_map/all_to_all | solution.py:250
  158.2 0.0 copy-start
  158.2 0.0 copy-start.2
  158.2 0.0 copy-start.3
  158.2 15.6 %all_to_all.53.parts_ref = f32[32,24,128]{2,1,0:T(8,128)S(1)} all-to-all(f32[32,24,128]{2,1,0:T(8,128)S(1)} %shard_map.109), channel_id=1, replica_groups=mesh['x'=4,'zl'=8,'y'=4,'zh'=2,'co'=2] {'x','y','co'}, dimensions={0} | all-to-all | bytes 786432 | tf_op jit(solution)/shard_map/all_to_all | solution.py:250
  173.8 0.0 copy-done
  173.9 0.0 copy-done.2
  173.9 0.0 copy-done.3
  173.9 1.3 shard_map.110
  (2 shorter events, 0.1 us)
Async XLA Ops:
  57.3 14.5 %copy-start.6 = (f32[128,128]{1,0:T(8,128)S(1)}, f32[128,128]{1,0:T(8,128)}, u32[]{:S(2)}) copy-start(f32[128,128]{1,0:T(8,128)} %wout_ref.3) | copy-start | bytes 196612
  57.4 14.4 %copy-start.1 = (f32[128,128]{1,0:T(8,128)S(1)}, f32[128,128]{1,0:T(8,128)}, u32[]{:S(2)}) copy-start(f32[128,128]{1,0:T(8,128)} %get-tuple-element.25.gate_ref) | copy-start | bytes 196612
  57.4 14.4 %copy-start.5 = (f32[8,16,128]{2,1,0:T(8,128)S(1)}, f32[8,16,128]{2,1,0:T(8,128)}, u32[]{:S(2)}) copy-start(f32[8,16,128]{2,1,0:T(8,128)} %cot_ref.3) | copy-start | bytes 196612
  102.0 24.5 %copy-start.7 = (f32[128,128]{1,0:T(8,128)S(1)}, f32[128,128]{1,0:T(8,128)}, u32[]{:S(2)}) copy-start(f32[128,128]{1,0:T(8,128)} %get-tuple-element.30.normed_ref) | copy-start | bytes 196612
  103.2 23.3 %copy-start.4 = (f32[512,128]{1,0:T(8,128)S(1)}, f32[512,128]{1,0:T(8,128)}, u32[]{:S(2)}) copy-start(f32[512,128]{1,0:T(8,128)} %get-tuple-element.29.factor_ref) | copy-start | bytes 786436
  158.2 15.6 %copy-start = (f32[128,512]{1,0:T(8,128)S(1)}, f32[128,512]{1,0:T(8,128)}, u32[]{:S(2)}) copy-start(f32[128,512]{1,0:T(8,128)} %win_ref.1) | copy-start | bytes 786436
  158.2 15.6 %copy-start.2 = (f32[8,16,128]{2,1,0:T(8,128)S(1)}, f32[8,16,128]{2,1,0:T(8,128)}, u32[]{:S(2)}) copy-start(f32[8,16,128]{2,1,0:T(8,128)} %pair_ref.1) | copy-start | bytes 196612
  158.2 15.6 %copy-start.3 = (f32[128,128]{1,0:T(8,128)S(1)}, f32[128,128]{1,0:T(8,128)}, u32[]{:S(2)}) copy-start(f32[128,128]{1,0:T(8,128)} %wgate_ref.1) | copy-start | bytes 196612

commit v7 on v6

--- a/solution.py
+++ b/solution.py
@@ -7,7 +7,7 @@
 
 ROW = ("x", "zl")
 CH = ("y", "zh", "co")
-CHANNELS = ("zh", "zl", "co", "x")
+CHANNELS = ("zh", "zl", "x", "co")
 PLANE = ("x", "y", "co")
 DEPTH = ("zh", "zl")
 F32 = jnp.float32
@@ -95,7 +95,7 @@
     flat_ref[0, 0:128] = msg_ref[:, 0, 0:128]
     flat_ref[1, 0:128] = msg_ref[:, 0, 128:256]
     for x, co, zh in channel_blocks():
-        source, lanes = pl.ds(zh * 64 + co * 4 + x, 8, stride=8), slice(zh * 32 + co * 16, zh * 32 + co * 16 + 16)
+        source, lanes = pl.ds(zh * 64 + x * 2 + co, 8, stride=8), slice(zh * 32 + co * 16, zh * 32 + co * 16 + 16)
         left, right = flat_ref[0, source, :], flat_ref[1, source, :]
         for s in range(8):
             left_ref[x * 64 + s * 8 : x * 64 + s * 8 + 8, lanes] = left[:, s * 16 : (s + 1) * 16]
@@ -121,7 +121,7 @@
 def home_kernel(part_ref, msg_ref, rows_ref):
     for co in range(2):
         for x in range(4):
-            at, to = x * 8 + co, (co * 4 + x) * 16
+            at, to = x * 8 + co, (x * 2 + co) * 16
             rows_ref[to : to + 16, :] = (part_ref[at] + part_ref[at + 2]) + (part_ref[at + 4] + part_ref[at + 6])
     rows_ref[0:128] = rows_ref[0:128].T
     for zl in range(8):
@@ -169,7 +169,7 @@
     turned = rows_ref[...].T
     for x in range(4):
         for co in range(2):
-            block = turned[(co * 4 + x) * 16 : (co * 4 + x) * 16 + 16]
+            block = turned[(x * 2 + co) * 16 : (x * 2 + co) * 16 + 16]
             for y in range(4):
                 out_ref[(x * 4 + y) * 2 + co] = block
 
@@ -196,7 +196,7 @@
             turn_ref[1, co, zh, x, :, to] = d_right[x * 8 : (x + 1) * 8, lanes]
     for side in range(2):
         for x, co, zh in channel_blocks():
-            flat_ref[side, pl.ds(zh * 64 + co * 4 + x, 8, stride=8), :] = turn_ref[side, co, zh, x]
+            flat_ref[side, pl.ds(zh * 64 + x * 2 + co, 8, stride=8), :] = turn_ref[side, co, zh, x]
         msg_ref[:, 0, side * 128 : (side + 1) * 128] = flat_ref[side, 0:128]
 
 

time: 176 us -> 176 us (level)
  no operation moved by 1% of the time
where the time goes in v7:
time: 176 us; the launch traced here: 175 us
  blocking collectives  167 us (95%)
  Pallas kernels  7.57 us (4%)
    all_to_all x9, blocking collectives, swap(): return lax.all_to_all(values, axes, split_axis=0, concat_axis=0, tiled=True)  167 us
    pallas_call x9, Pallas kernels, run(): pl.pallas_call(body, out_shape=[jax.ShapeDtypeStruct(s, F32) for s in out...  5 us

profile of v7, /device:TPU:1, one launch (start us, length us, event | category | flops | bytes accessed | tf_op | source)
XLA Modules:
  0.0 175.1 jit_solution(14049983443029461771)
XLA Ops:
  0.6 2.6 %shard_map.101 = (f32[128,1,256]{2,1,0:T(1,128)}, f32[512,128]{1,0:T(8,128)}, f32[128,128]{1,0:T(8,128)}, f32[128,128]{1,0:T(8,128)}) custom-call(f32[8,16,128]{2,1,0:T(8,128)} %pair_ref.1, s32[8,16]{1,0:T(8,128)} %mask_hbm.1, f32[128,512]{1,0:T(8,128)} %win_ref.1, f32[128,128]{1,0:T(8,128)} %wgate_ref.1), custom_call_target="tpu_custom_call" | custom-call | tf_op jit(solution)/shard_map/pallas_call | solution.py:255
  3.2 36.5 %all_to_all.45.msg_ref = f32[128,1,256]{2,1,0:T(1,128)S(1)} all-to-all(f32[128,1,256]{2,1,0:T(1,128)} %get-tuple-element.23), channel_id=1, replica_groups=mesh['x'=4,'zl'=8,'y'=4,'zh'=2,'co'=2] {'zh','zl','x','co'}, dimensions={0} | all-to-all | bytes 262144 | tf_op jit(solution)/shard_map/all_to_all | solution.py:250
  39.7 0.8 shard_map.102
  40.5 16.3 %all_to_all.46.part_ref = f32[32,16,128]{2,1,0:T(8,128)S(1)} all-to-all(f32[32,16,128]{2,1,0:T(8,128)S(1)} %get-tuple-element.24), channel_id=1, replica_groups=mesh['x'=4,'zl'=8,'y'=4,'zh'=2,'co'=2] {'x','y','co'}, dimensions={0} | all-to-all | bytes 524288 | tf_op jit(solution)/shard_map/all_to_all | solution.py:250
  56.8 0.0 copy-start.6
  56.8 0.1 shard_map.103
  56.9 0.0 copy-start.1
  57.0 0.0 copy-start.5
  57.0 14.4 %all_to_all.47.home_ref = f32[16,8,128]{2,1,0:T(8,128)S(1)} all-to-all(f32[16,8,128]{2,1,0:T(8,128)S(1)} %shard_map.103), channel_id=1, replica_groups=mesh['x'=4,'zl'=8,'y'=4,'zh'=2,'co'=2] {'zh','zl'}, dimensions={0} | all-to-all | bytes 131072 | tf_op jit(solution)/shard_map/all_to_all | solution.py:250
  71.4 0.0 copy-done.6
  71.4 0.0 copy-done.1
  71.4 0.0 copy-done.5
  71.4 0.5 shard_map.104
  71.9 15.2 %all_to_all.48.msg_ref = f32[16,8,128]{2,1,0:T(8,128)S(1)} all-to-all(f32[16,8,128]{2,1,0:T(8,128)S(1)} %get-tuple-element.26), channel_id=1, replica_groups=mesh['x'=4,'zl'=8,'y'=4,'zh'=2,'co'=2] {'zh','zl'}, dimensions={0} | all-to-all | bytes 131072 | tf_op jit(solution)/shard_map/all_to_all | solution.py:250
  87.1 0.1 shard_map.105
  87.2 14.4 %all_to_all.49.dtri_ref = f32[32,16,128]{2,1,0:T(8,128)S(1)} all-to-all(f32[32,16,128]{2,1,0:T(8,128)S(1)} %shard_map.105), channel_id=1, replica_groups=mesh['x'=4,'zl'=8,'y'=4,'zh'=2,'co'=2] {'x','y','co'}, dimensions={0} | all-to-all | bytes 524288 | tf_op jit(solution)/shard_map/all_to_all | solution.py:250
  101.6 0.0 copy-start.7
  101.6 1.2 shard_map.106
  102.8 0.0 copy-start.4
  102.8 21.6 %all_to_all.50.msg_ref = f32[128,1,256]{2,1,0:T(1,128)S(1)} all-to-all(f32[128,1,256]{2,1,0:T(1,128)S(1)} %shard_map.106), channel_id=1, replica_groups=mesh['x'=4,'zl'=8,'y'=4,'zh'=2,'co'=2] {'zh','zl','x','co'}, dimensions={0} | all-to-all | bytes 262144 | tf_op jit(solution)/shard_map/all_to_all | solution.py:250
  124.4 0.0 copy-done.7
  124.4 0.0 copy-done.4
  124.4 0.9 shard_map.107
  125.2 15.4 %all_to_all.51.a = f32[32,24,128]{2,1,0:T(8,128)S(1)} all-to-all(f32[32,24,128]{2,1,0:T(8,128)S(1)} %bitcast.1), channel_id=1, replica_groups=mesh['x'=4,'zl'=8,'y'=4,'zh'=2,'co'=2] {'x','y','co'}, dimensions={0} | all-to-all | bytes 786432 | tf_op jit(solution)/shard_map/all_to_all | solution.py:250
  140.7 15.8 %all_to_all.52.a = f32[16,24,128]{2,1,0:T(8,128)S(1)} all-to-all(f32[16,24,128]{2,1,0:T(8,128)S(1)} %shard_map.108), channel_id=1, replica_groups=mesh['x'=4,'zl'=8,'y'=4,'zh'=2,'co'=2] {'zh','zl'}, dimensions={0} | all-to-all | bytes 393216 | tf_op jit(solution)/shard_map/all_to_all | solution.py:250
  156.5 0.0 copy-start
  156.5 0.0 copy-start.2
  156.6 0.0 copy-start.3
  156.6 17.2 %all_to_all.53.parts_ref = f32[32,24,128]{2,1,0:T(8,128)S(1)} all-to-all(f32[32,24,128]{2,1,0:T(8,128)S(1)} %shard_map.109), channel_id=1, replica_groups=mesh['x'=4,'zl'=8,'y'=4,'zh'=2,'co'=2] {'x','y','co'}, dimensions={0} | all-to-all | bytes 786432 | tf_op jit(solution)/shard_map/all_to_all | solution.py:250
  173.8 0.0 copy-done
  173.8 0.0 copy-done.2
  173.8 0.0 copy-done.3
  173.8 1.3 shard_map.110
  (2 shorter events, 0.1 us)
Async XLA Ops:
  56.8 14.6 %copy-start.6 = (f32[128,128]{1,0:T(8,128)S(1)}, f32[128,128]{1,0:T(8,128)}, u32[]{:S(2)}) copy-start(f32[128,128]{1,0:T(8,128)} %wout_ref.3) | copy-start | bytes 196612
  56.9 14.4 %copy-start.1 = (f32[128,128]{1,0:T(8,128)S(1)}, f32[128,128]{1,0:T(8,128)}, u32[]{:S(2)}) copy-start(f32[128,128]{1,0:T(8,128)} %get-tuple-element.25.gate_ref) | copy-start | bytes 196612
  57.0 14.4 %copy-start.5 = (f32[8,16,128]{2,1,0:T(8,128)S(1)}, f32[8,16,128]{2,1,0:T(8,128)}, u32[]{:S(2)}) copy-start(f32[8,16,128]{2,1,0:T(8,128)} %cot_ref.3) | copy-start | bytes 196612
  101.6 22.8 %copy-start.7 = (f32[128,128]{1,0:T(8,128)S(1)}, f32[128,128]{1,0:T(8,128)}, u32[]{:S(2)}) copy-start(f32[128,128]{1,0:T(8,128)} %get-tuple-element.30.normed_ref) | copy-start | bytes 196612
  102.8 21.6 %copy-start.4 = (f32[512,128]{1,0:T(8,128)S(1)}, f32[512,128]{1,0:T(8,128)}, u32[]{:S(2)}) copy-start(f32[512,128]{1,0:T(8,128)} %get-tuple-element.29.factor_ref) | copy-start | bytes 786436
  156.5 17.2 %copy-start = (f32[128,512]{1,0:T(8,128)S(1)}, f32[128,512]{1,0:T(8,128)}, u32[]{:S(2)}) copy-start(f32[128,512]{1,0:T(8,128)} %win_ref.1) | copy-start | bytes 786436
  156.5 17.2 %copy-start.2 = (f32[8,16,128]{2,1,0:T(8,128)S(1)}, f32[8,16,128]{2,1,0:T(8,128)}, u32[]{:S(2)}) copy-start(f32[8,16,128]{2,1,0:T(8,128)} %pair_ref.1) | copy-start | bytes 196612
  156.6 17.2 %copy-start.3 = (f32[128,128]{1,0:T(8,128)S(1)}, f32[128,128]{1,0:T(8,128)}, u32[]{:S(2)}) copy-start(f32[128,128]{1,0:T(8,128)} %wgate_ref.1) | copy-start | bytes 196612

commit v8 on v7

--- a/solution.py
+++ b/solution.py
@@ -67,11 +67,11 @@
     copies[1].wait()
     maskf = mask_lanes(mask_ref, lanes_ref)
     copies[2].wait()
-    proj = dot(win_ref[...], normed, 0, 1)
     for side in range(2):
         base = side * 256
-        value = proj[base + 128 : base + 256]
-        sig = jax.nn.sigmoid(proj[base : base + 128])
+        proj = dot(win_ref[:, base : base + 256], normed, 0, 1)
+        value = proj[128:256]
+        sig = jax.nn.sigmoid(proj[0:128])
         masked = maskf * sig
         msg_ref[:, 0, side * 128 : (side + 1) * 128] = masked * value
         factor_ref[base : base + 128] = masked
@@ -87,35 +87,36 @@
 
 def column_blocks():
     return [
-        (y * 64 + co * 32 + zh * 16, y * 64 + zh * 32 + co * 16) for y in range(4) for co in range(2) for zh in range(2)
+        ((y * 2 + co) * 16, zh * 64, y * 64 + zh * 32 + co * 16)
+        for y in range(4) for co in range(2) for zh in range(2)
     ]
 
 
-def triangle_kernel(msg_ref, part_ref, left_ref, right_ref, flat_ref, turn_ref, natural_ref):
+def channel_blocks():
+    return [(x, co, zh) for x in range(4) for co in range(2) for zh in range(2)]
+
+
+def triangle_kernel(msg_ref, part_ref, left_ref, right_ref, flat_ref, rows_ref, turn_ref, natural_ref):
     flat_ref[0, 0:128] = msg_ref[:, 0, 0:128]
     flat_ref[1, 0:128] = msg_ref[:, 0, 128:256]
     for x, co, zh in channel_blocks():
         source, lanes = pl.ds(zh * 64 + x * 2 + co, 8, stride=8), slice(zh * 32 + co * 16, zh * 32 + co * 16 + 16)
         left, right = flat_ref[0, source, :], flat_ref[1, source, :]
         for s in range(8):
-            left_ref[x * 64 + s * 8 : x * 64 + s * 8 + 8, lanes] = left[:, s * 16 : (s + 1) * 16]
+            rows_ref[x * 64 + s * 8 : x * 64 + s * 8 + 8, lanes] = left[:, s * 16 : (s + 1) * 16]
             turn_ref[s * 32 + x * 8 : s * 32 + x * 8 + 8, lanes] = right[:, s * 16 : (s + 1) * 16]
     for s in range(8):
         natural_ref[pl.ds(s, 32, stride=8), :] = turn_ref[s * 32 : (s + 1) * 32, :]
-    for to, at in column_blocks():
-        right_ref[to : to + 16, :] = natural_ref[at : at + 16, :]
+    for row, lane, at in column_blocks():
+        right_ref[row : row + 16, lane : lane + 64] = natural_ref[at : at + 16, :]
+    left_ref[...] = jnp.zeros((512, 128), F32)
+    for x in range(4):
+        block = rows_ref[x * 64 : (x + 1) * 64, :]
+        left_ref[x * 128 : x * 128 + 64, 0:64] = block
+        left_ref[x * 128 + 64 : x * 128 + 128, 64:128] = block
     part = dot(right_ref[...], left_ref[...], 1, 1)
-    for x, y, co, zh in plane_blocks():
-        row = y * 64 + co * 32 + zh * 16
-        part_ref[(x * 4 + y) * 2 + co, :, zh * 64 : (zh + 1) * 64] = part[row : row + 16, x * 64 : (x + 1) * 64]
-
-
-def channel_blocks():
-    return [(x, co, zh) for x in range(4) for co in range(2) for zh in range(2)]
-
-
-def plane_blocks():
-    return [(x, y, co, zh) for x in range(4) for y in range(4) for co in range(2) for zh in range(2)]
+    for x in range(4):
+        part_ref[x * 8 : (x + 1) * 8] = part[:, x * 128 : (x + 1) * 128].reshape(8, 16, 128)
 
 
 def home_kernel(part_ref, msg_ref, rows_ref):
@@ -174,25 +175,22 @@
                 out_ref[(x * 4 + y) * 2 + co] = block
 
 
-def back_kernel(
-    dtri_ref, left_ref, right_ref, msg_ref, whole_ref, flat_ref, blocks_ref, natural_ref, turn_ref
-):
-    for x, y, co, zh in plane_blocks():
-        row = y * 64 + co * 32 + zh * 16
-        whole_ref[row : row + 16, x * 64 : (x + 1) * 64] = dtri_ref[
-            (x * 4 + y) * 2 + co, :, zh * 64 : (zh + 1) * 64
-        ]
-    dtri = whole_ref[...]
-    blocks_ref[...] = dot(dtri, left_ref[...], 1, 0)
-    d_left = dot(right_ref[...], dtri, 0, 0).T
-    for at, to in column_blocks():
-        natural_ref[to : to + 16, :] = blocks_ref[at : at + 16, :]
+def back_kernel(dtri_ref, left_ref, right_ref, msg_ref, flat_ref, rows_ref, natural_ref, turn_ref):
+    right = right_ref[...]
+    total = jnp.zeros((128, 128), F32)
+    for x in range(4):
+        block = dtri_ref[x * 8 : (x + 1) * 8].reshape(128, 128)
+        total += dot(block, left_ref[x * 128 : (x + 1) * 128], 1, 0)
+        both = dot(block, right, 0, 0)
+        rows_ref[x * 64 : (x + 1) * 64, :] = both[0:64, 0:64] + both[64:128, 64:128]
+    for row, lane, at in column_blocks():
+        natural_ref[at : at + 16, :] = total[row : row + 16, lane : lane + 64]
     for s in range(8):
         d_right = natural_ref[pl.ds(s, 32, stride=8), :]
         to = slice(s * 16, (s + 1) * 16)
         for x, co, zh in channel_blocks():
             lanes = slice(zh * 32 + co * 16, zh * 32 + co * 16 + 16)
-            turn_ref[0, co, zh, x, :, to] = d_left[x * 64 + s * 8 : x * 64 + s * 8 + 8, lanes]
+            turn_ref[0, co, zh, x, :, to] = rows_ref[x * 64 + s * 8 : x * 64 + s * 8 + 8, lanes]
             turn_ref[1, co, zh, x, :, to] = d_right[x * 8 : (x + 1) * 8, lanes]
     for side in range(2):
         for x, co, zh in channel_blocks():
@@ -232,18 +230,26 @@
 
 def leave_kernel(
     parts_ref, dproj_ref, dpre_ref, out_ref, gate_ref, pair_ref, win_ref, wgate_ref,
-    dpair_ref, upd_ref, dwin_ref, dwg_ref, dwo_ref
+    dpair_hbm, upd_hbm, dwin_hbm, dwg_hbm, dwo_hbm, dpair_ref, upd_ref, sems
 ):
-    for f in range(4):
-        dwin_ref[:, f * 128 : (f + 1) * 128] = parts_ref[...].reshape(768, 128)[f * 128 : (f + 1) * 128]
-    dwg_ref[...] = parts_ref[...].reshape(768, 128)[512:640]
-    dwo_ref[...] = parts_ref[...].reshape(768, 128)[640:768]
+    pairs = [
+        (parts_ref.at[pl.ds(f * 128, 128), :], dwin_hbm.at[:, pl.ds(f * 128, 128)]) for f in range(4)
+    ]
+    pairs += [(parts_ref.at[pl.ds(512, 128), :], dwg_hbm), (parts_ref.at[pl.ds(640, 128), :], dwo_hbm)]
+    pairs += [(upd_ref, upd_hbm), (dpair_ref, dpair_hbm)]
+    copies = [pltpu.make_async_copy(source, target, sems.at[i]) for i, (source, target) in enumerate(pairs)]
+    for copy in copies[:6]:
+        copy.start()
     upd_ref[...] = (gate_ref[...] * out_ref[...]).reshape(8, 16, 128)
+    copies[6].start()
     normed, rstd = norm_rows(pair_ref[...].reshape(128, 128))
     d_normed = dot(dproj_ref[...], win_ref[...], 0, 1) + dot(dpre_ref[...], wgate_ref[...], 1, 1)
     along = jnp.mean(d_normed * normed, axis=1, keepdims=True)
     d_pair = rstd * (d_normed - jnp.mean(d_normed, axis=1, keepdims=True) - normed * along)
     dpair_ref[...] = d_pair.reshape(8, 16, 128)
+    copies[7].start()
+    for copy in copies:
+        copy.wait()
 
 
 def swap(values, axes):
@@ -271,13 +277,25 @@
     )(pair, pair_mask, w_in, w_gate)
 
 
+def leave(*args):
+    outs = [(8, 16, 128), (8, 16, 128), (128, 512), (128, 128), (128, 128)]
+    return pl.pallas_call(
+        leave_kernel,
+        out_shape=[jax.ShapeDtypeStruct(s, F32) for s in outs],
+        in_specs=[pl.BlockSpec(memory_space=pltpu.VMEM)] * len(args),
+        out_specs=[pl.BlockSpec(memory_space=pl.ANY)] * len(outs),
+        scratch_shapes=[pltpu.VMEM(outs[0], F32), pltpu.VMEM(outs[1], F32), pltpu.SemaphoreType.DMA((8,))],
+        compiler_params=pltpu.CompilerParams(vmem_limit_bytes=32 * 1024 * 1024),
+    )(*args)
+
+
 def shards(pair, pair_mask, w_in, w_gate, w_out, cotangent):
     msg, factor, normed, gate = enter(pair, pair_mask, w_in, w_gate)
     msg = swap(msg, CHANNELS)
     part, left, right = call(
         triangle_kernel,
-        [(32, 16, 128), (256, 64), (256, 64)],
-        [(2, 144, 128), (256, 64), (264, 64)],
+        [(32, 16, 128), (512, 128), (128, 128)],
+        [(2, 144, 128), (256, 64), (256, 64), (264, 64)],
     )(msg)
     part = swap(part, PLANE)
     (msg,) = call(home_kernel, [(16, 8, 128)], [(136, 128)])(part)
@@ -291,7 +309,7 @@
     (msg,) = call(
         back_kernel,
         [(128, 1, 256)],
-        [(256, 256), (2, 144, 128), (256, 64), (264, 64), (2, 2, 2, 4, 8, 128)],
+        [(2, 144, 128), (256, 64), (264, 64), (2, 2, 2, 4, 8, 128)],
     )(d_tri, left, right)
     msg = swap(msg, CHANNELS)
     weights, d_proj, d_pre, out_proj = call(
@@ -303,9 +321,9 @@
     scale = 1.0 / (pair.shape[0] * lax.axis_size(ROW))
     (parts,) = call(lambda a, b: sum_kernel(scale, a, b), [(32, 24, 128)])(parts)
     parts = swap(parts, PLANE)
-    d_pair, update, d_win, d_wgate, d_wout = call(
-        leave_kernel, [(8, 16, 128), (8, 16, 128), (128, 512), (128, 128), (128, 128)]
-    )(parts, d_proj, d_pre, out_proj, gate, pair, w_in, w_gate)
+    d_pair, update, d_win, d_wgate, d_wout = leave(
+        parts.reshape(768, 128), d_proj, d_pre, out_proj, gate, pair, w_in, w_gate
+    )
     return (update, d_pair, d_win, d_wgate, d_wout)
 
 

time: 176 us -> 175 us (level)
    pallas_call x9 -> x8, Pallas kernels: 5 us -> 3.61 us  [run(): pl.pallas_call(body, out_shape=[jax.ShapeDtypeStruct(s, F32) for s in out...]
where the time goes in v8:
time: 175 us
  blocking collectives  167 us (95%)
  Pallas kernels  7.44 us (4%)
    all_to_all x9, blocking collectives, swap(): return lax.all_to_all(values, axes, split_axis=0, concat_axis=0, tiled=True)  167 us
    pallas_call x8, Pallas kernels, run(): pl.pallas_call(body, out_shape=[jax.ShapeDtypeStruct(s, F32) for s in out...  3.61 us

profile of v8, /device:TPU:1, one launch (start us, length us, event | category | flops | bytes accessed | tf_op | source)
XLA Modules:
  0.0 175.0 jit_solution(536555017311619246)
XLA Ops:
  0.6 2.5 %shard_map.101 = (f32[128,1,256]{2,1,0:T(1,128)}, f32[512,128]{1,0:T(8,128)}, f32[128,128]{1,0:T(8,128)}, f32[128,128]{1,0:T(8,128)}) custom-call(f32[8,16,128]{2,1,0:T(8,128)} %pair_ref.1, s32[8,16]{1,0:T(8,128)} %mask_hbm.1, f32[128,512]{1,0:T(8,128)} %win_ref.1, f32[128,128]{1,0:T(8,128)} %wgate_ref.1), custom_call_target="tpu_custom_call" | custom-call | tf_op jit(solution)/shard_map/pallas_call | solution.py:261
  3.2 36.5 %all_to_all.45.msg_ref = f32[128,1,256]{2,1,0:T(1,128)S(1)} all-to-all(f32[128,1,256]{2,1,0:T(1,128)} %get-tuple-element.23), channel_id=1, replica_groups=mesh['x'=4,'zl'=8,'y'=4,'zh'=2,'co'=2] {'zh','zl','x','co'}, dimensions={0} | all-to-all | bytes 262144 | tf_op jit(solution)/shard_map/all_to_all | solution.py:256
  39.7 0.8 shard_map.102
  40.5 16.3 %all_to_all.46.part_ref = f32[32,16,128]{2,1,0:T(8,128)S(1)} all-to-all(f32[32,16,128]{2,1,0:T(8,128)S(1)} %get-tuple-element.24), channel_id=1, replica_groups=mesh['x'=4,'zl'=8,'y'=4,'zh'=2,'co'=2] {'x','y','co'}, dimensions={0} | all-to-all | bytes 524288 | tf_op jit(solution)/shard_map/all_to_all | solution.py:256
  56.8 0.0 copy-start.6
  56.8 0.1 shard_map.103
  56.9 0.0 copy-start.1
  56.9 0.0 copy-start.5
  56.9 14.4 %all_to_all.47.home_ref = f32[16,8,128]{2,1,0:T(8,128)S(1)} all-to-all(f32[16,8,128]{2,1,0:T(8,128)S(1)} %shard_map.103), channel_id=1, replica_groups=mesh['x'=4,'zl'=8,'y'=4,'zh'=2,'co'=2] {'zh','zl'}, dimensions={0} | all-to-all | bytes 131072 | tf_op jit(solution)/shard_map/all_to_all | solution.py:256
  71.4 0.0 copy-done.6
  71.4 0.0 copy-done.1
  71.4 0.0 copy-done.5
  71.4 0.5 shard_map.104
  71.9 15.2 %all_to_all.48.msg_ref = f32[16,8,128]{2,1,0:T(8,128)S(1)} all-to-all(f32[16,8,128]{2,1,0:T(8,128)S(1)} %get-tuple-element.26), channel_id=1, replica_groups=mesh['x'=4,'zl'=8,'y'=4,'zh'=2,'co'=2] {'zh','zl'}, dimensions={0} | all-to-all | bytes 131072 | tf_op jit(solution)/shard_map/all_to_all | solution.py:256
  87.1 0.1 shard_map.105
  87.2 14.4 %all_to_all.49.dtri_ref = f32[32,16,128]{2,1,0:T(8,128)S(1)} all-to-all(f32[32,16,128]{2,1,0:T(8,128)S(1)} %shard_map.105), channel_id=1, replica_groups=mesh['x'=4,'zl'=8,'y'=4,'zh'=2,'co'=2] {'x','y','co'}, dimensions={0} | all-to-all | bytes 524288 | tf_op jit(solution)/shard_map/all_to_all | solution.py:256
  101.6 0.0 copy-start.7
  101.6 1.1 shard_map.106
  102.7 0.0 copy-start.4
  102.7 21.6 %all_to_all.50.msg_ref = f32[128,1,256]{2,1,0:T(1,128)S(1)} all-to-all(f32[128,1,256]{2,1,0:T(1,128)S(1)} %shard_map.106), channel_id=1, replica_groups=mesh['x'=4,'zl'=8,'y'=4,'zh'=2,'co'=2] {'zh','zl','x','co'}, dimensions={0} | all-to-all | bytes 262144 | tf_op jit(solution)/shard_map/all_to_all | solution.py:256
  124.2 0.0 copy-done.7
  124.3 0.0 copy-done.4
  124.3 0.9 shard_map.107
  125.1 15.4 %all_to_all.51.a = f32[32,24,128]{2,1,0:T(8,128)S(1)} all-to-all(f32[32,24,128]{2,1,0:T(8,128)S(1)} %bitcast.3), channel_id=1, replica_groups=mesh['x'=4,'zl'=8,'y'=4,'zh'=2,'co'=2] {'x','y','co'}, dimensions={0} | all-to-all | bytes 786432 | tf_op jit(solution)/shard_map/all_to_all | solution.py:256
  140.5 15.8 %all_to_all.52.a = f32[16,24,128]{2,1,0:T(8,128)S(1)} all-to-all(f32[16,24,128]{2,1,0:T(8,128)S(1)} %shard_map.108), channel_id=1, replica_groups=mesh['x'=4,'zl'=8,'y'=4,'zh'=2,'co'=2] {'zh','zl'}, dimensions={0} | all-to-all | bytes 393216 | tf_op jit(solution)/shard_map/all_to_all | solution.py:256
  156.4 0.0 copy-start
  156.4 0.0 copy-start.2
  156.4 0.0 copy-start.3
  156.4 17.2 %all_to_all.53 = f32[32,24,128]{2,1,0:T(8,128)S(1)} all-to-all(f32[32,24,128]{2,1,0:T(8,128)S(1)} %shard_map.109), channel_id=1, replica_groups=mesh['x'=4,'zl'=8,'y'=4,'zh'=2,'co'=2] {'x','y','co'}, dimensions={0} | all-to-all | bytes 786432 | tf_op jit(solution)/shard_map/all_to_all | solution.py:256
  173.7 0.0 copy-done
  173.7 0.0 copy-done.2
  173.7 0.0 copy-done.3
  173.7 1.3 shard_map.110
  (2 shorter events, 0.1 us)
Async XLA Ops:
  56.8 14.6 %copy-start.6 = (f32[128,128]{1,0:T(8,128)S(1)}, f32[128,128]{1,0:T(8,128)}, u32[]{:S(2)}) copy-start(f32[128,128]{1,0:T(8,128)} %wout_ref.3) | copy-start | bytes 196612
  56.9 14.4 %copy-start.1 = (f32[128,128]{1,0:T(8,128)S(1)}, f32[128,128]{1,0:T(8,128)}, u32[]{:S(2)}) copy-start(f32[128,128]{1,0:T(8,128)} %get-tuple-element.25.gate_ref) | copy-start | bytes 196612
  56.9 14.4 %copy-start.5 = (f32[8,16,128]{2,1,0:T(8,128)S(1)}, f32[8,16,128]{2,1,0:T(8,128)}, u32[]{:S(2)}) copy-start(f32[8,16,128]{2,1,0:T(8,128)} %cot_ref.3) | copy-start | bytes 196612
  101.6 22.7 %copy-start.7 = (f32[128,128]{1,0:T(8,128)S(1)}, f32[128,128]{1,0:T(8,128)}, u32[]{:S(2)}) copy-start(f32[128,128]{1,0:T(8,128)} %get-tuple-element.30.normed_ref) | copy-start | bytes 196612
  102.7 21.6 %copy-start.4 = (f32[512,128]{1,0:T(8,128)S(1)}, f32[512,128]{1,0:T(8,128)}, u32[]{:S(2)}) copy-start(f32[512,128]{1,0:T(8,128)} %get-tuple-element.29.factor_ref) | copy-start | bytes 786436
  156.4 17.2 %copy-start = (f32[128,512]{1,0:T(8,128)S(1)}, f32[128,512]{1,0:T(8,128)}, u32[]{:S(2)}) copy-start(f32[128,512]{1,0:T(8,128)} %win_ref.1) | copy-start | bytes 786436
  156.4 17.2 %copy-start.2 = (f32[8,16,128]{2,1,0:T(8,128)S(1)}, f32[8,16,128]{2,1,0:T(8,128)}, u32[]{:S(2)}) copy-start(f32[8,16,128]{2,1,0:T(8,128)} %pair_ref.1) | copy-start | bytes 196612
  156.4 17.2 %copy-start.3 = (f32[128,128]{1,0:T(8,128)S(1)}, f32[128,128]{1,0:T(8,128)}, u32[]{:S(2)}) copy-start(f32[128,128]{1,0:T(8,128)} %wgate_ref.1) | copy-start | bytes 196612

commit v9 on v8

--- a/solution.py
+++ b/solution.py
@@ -50,23 +50,17 @@
     return lanes_ref[0:1, :]
 
 
+def clear_kernel(lanes_ref):
+    lanes_ref[...] = jnp.zeros((8, 128), F32)
+
+
 def enter_kernel(
-    pair_hbm, mask_hbm, win_hbm, wgate_hbm, msg_hbm, factor_hbm, normed_hbm, gate_hbm,
-    pair_ref, mask_ref, win_ref, wgate_ref, msg_ref, factor_ref, normed_ref, gate_ref, lanes_ref, ins, outs
+    lanes_in, pair_ref, mask_ref, win_ref, wgate_ref, msg_ref, factor_ref, normed_ref, gate_ref, lanes_ref
 ):
-    pairs = ((pair_hbm, pair_ref), (mask_hbm, mask_ref), (win_hbm, win_ref), (wgate_hbm, wgate_ref))
-    copies = [pltpu.make_async_copy(source, target, ins.at[i]) for i, (source, target) in enumerate(pairs)]
-    pairs = ((msg_ref, msg_hbm), (factor_ref, factor_hbm), (normed_ref, normed_hbm), (gate_ref, gate_hbm))
-    results = [pltpu.make_async_copy(source, target, outs.at[i]) for i, (source, target) in enumerate(pairs)]
-    for copy in copies:
-        copy.start()
-    copies[0].wait()
+    lanes_ref[...] = lanes_in[...]
     normed, _ = norm_rows(pair_ref[...].reshape(128, 128))
     normed_ref[...] = normed
-    results[2].start()
-    copies[1].wait()
     maskf = mask_lanes(mask_ref, lanes_ref)
-    copies[2].wait()
     for side in range(2):
         base = side * 256
         proj = dot(win_ref[:, base : base + 256], normed, 0, 1)
@@ -76,13 +70,7 @@
         msg_ref[:, 0, side * 128 : (side + 1) * 128] = masked * value
         factor_ref[base : base + 128] = masked
         factor_ref[base + 128 : base + 256] = value * (1.0 - sig)
-    results[0].start()
-    results[1].start()
-    copies[3].wait()
     gate_ref[...] = jax.nn.sigmoid(dot(normed, wgate_ref[...], 1, 0))
-    results[3].start()
-    for result in results:
-        result.wait()
 
 
 def column_blocks():
@@ -257,24 +245,15 @@
 
 
 def enter(pair, pair_mask, w_in, w_gate):
+    lanes = pl.pallas_call(
+        clear_kernel,
+        out_shape=jax.ShapeDtypeStruct((8, 128), F32),
+        out_specs=pl.BlockSpec(memory_space=pltpu.VMEM),
+        cost_estimate=pl.CostEstimate(flops=10**10, bytes_accessed=2**25, transcendentals=0),
+        compiler_params=pltpu.CompilerParams(vmem_limit_bytes=4 * 1024 * 1024),
+    )()
     held = [(128, 1, 256), (512, 128), (128, 128), (128, 128)]
-    return pl.pallas_call(
-        enter_kernel,
-        out_shape=[jax.ShapeDtypeStruct(s, F32) for s in held],
-        in_specs=[pl.BlockSpec(memory_space=pl.ANY)] * 4,
-        out_specs=[pl.BlockSpec(memory_space=pl.ANY)] * 4,
-        scratch_shapes=[
-            pltpu.VMEM(pair.shape, F32),
-            pltpu.VMEM(pair_mask.shape, pair_mask.dtype),
-            pltpu.VMEM(w_in.shape, F32),
-            pltpu.VMEM(w_gate.shape, F32),
-            *[pltpu.VMEM(s, F32) for s in held],
-            pltpu.VMEM((8, 128), F32),
-            pltpu.SemaphoreType.DMA((4,)),
-            pltpu.SemaphoreType.DMA((4,)),
-        ],
-        compiler_params=pltpu.CompilerParams(vmem_limit_bytes=60 * 1024 * 1024),
-    )(pair, pair_mask, w_in, w_gate)
+    return call(enter_kernel, held, [(8, 128)])(lanes, pair, pair_mask, w_in, w_gate)
 
 
 def leave(*args):

time: 175 us -> 174 us (level)
  Pallas kernels: 7.44 us -> 5.53 us
    pallas_call x1, Pallas kernels: 2.52 us -> 0.01 us  [enter(): pl.pallas_call(clear_kernel, out_shape=jax.ShapeDtypeStruct((8, 128), F32...]
    pallas_call x8 -> x9, Pallas kernels: 3.61 us -> 4.23 us  [run(): pl.pallas_call(body, out_shape=[jax.ShapeDtypeStruct(s, F32) for s in out...]
where the time goes in v9:
time: 174 us; the launch traced here: 173 us
  blocking collectives  166 us (95%)
  Pallas kernels  5.53 us (3%)
    all_to_all x9, blocking collectives, swap(): return lax.all_to_all(values, axes, split_axis=0, concat_axis=0, tiled=True)  166 us
    pallas_call x9, Pallas kernels, run(): pl.pallas_call(body, out_shape=[jax.ShapeDtypeStruct(s, F32) for s in out...  4.23 us

profile of v9, /device:TPU:1, one launch (start us, length us, event | category | flops | bytes accessed | tf_op | source)
XLA Modules:
  0.0 173.5 jit_solution(4781797387892050896)
XLA Ops:
  0.6 0.0 copy-start.2
  0.6 0.0 copy-start
  0.7 0.0 copy-start.1
  0.7 0.0 copy-start.5
  0.7 0.8 copy-done.2
  1.5 0.1 copy-done
  1.6 0.0 copy-done.1
  1.6 0.0 copy-done.5
  1.6 0.6 shard_map.102
  2.3 36.6 %all_to_all.45.msg_ref = f32[128,1,256]{2,1,0:T(1,128)S(1)} all-to-all(f32[128,1,256]{2,1,0:T(1,128)S(1)} %get-tuple-element.23), channel_id=1, replica_groups=mesh['x'=4,'zl'=8,'y'=4,'zh'=2,'co'=2] {'zh','zl','x','co'}, dimensions={0} | all-to-all | bytes 262144 | tf_op jit(solution)/shard_map/all_to_all | solution.py:244
  38.9 0.8 shard_map.103
  39.7 16.0 %all_to_all.46.part_ref = f32[32,16,128]{2,1,0:T(8,128)S(1)} all-to-all(f32[32,16,128]{2,1,0:T(8,128)S(1)} %get-tuple-element.24), channel_id=1, replica_groups=mesh['x'=4,'zl'=8,'y'=4,'zh'=2,'co'=2] {'x','y','co'}, dimensions={0} | all-to-all | bytes 524288 | tf_op jit(solution)/shard_map/all_to_all | solution.py:244
  55.7 0.1 shard_map.104
  55.8 0.0 copy-start.3
  55.8 0.0 copy-start.4
  55.8 14.4 %all_to_all.47.home_ref = f32[16,8,128]{2,1,0:T(8,128)S(1)} all-to-all(f32[16,8,128]{2,1,0:T(8,128)S(1)} %shard_map.104), channel_id=1, replica_groups=mesh['x'=4,'zl'=8,'y'=4,'zh'=2,'co'=2] {'zh','zl'}, dimensions={0} | all-to-all | bytes 131072 | tf_op jit(solution)/shard_map/all_to_all | solution.py:244
  70.2 0.0 copy-done.3
  70.2 0.0 copy-done.4
  70.2 0.5 shard_map.105
  70.8 15.1 %all_to_all.48.msg_ref = f32[16,8,128]{2,1,0:T(8,128)S(1)} all-to-all(f32[16,8,128]{2,1,0:T(8,128)S(1)} %get-tuple-element.26), channel_id=1, replica_groups=mesh['x'=4,'zl'=8,'y'=4,'zh'=2,'co'=2] {'zh','zl'}, dimensions={0} | all-to-all | bytes 131072 | tf_op jit(solution)/shard_map/all_to_all | solution.py:244
  85.9 0.1 shard_map.106
  86.0 14.4 %all_to_all.49.dtri_ref = f32[32,16,128]{2,1,0:T(8,128)S(1)} all-to-all(f32[32,16,128]{2,1,0:T(8,128)S(1)} %shard_map.106), channel_id=1, replica_groups=mesh['x'=4,'zl'=8,'y'=4,'zh'=2,'co'=2] {'x','y','co'}, dimensions={0} | all-to-all | bytes 524288 | tf_op jit(solution)/shard_map/all_to_all | solution.py:244
  100.4 1.1 shard_map.107
  101.5 21.4 %all_to_all.50.msg_ref = f32[128,1,256]{2,1,0:T(1,128)S(1)} all-to-all(f32[128,1,256]{2,1,0:T(1,128)S(1)} %shard_map.107), channel_id=1, replica_groups=mesh['x'=4,'zl'=8,'y'=4,'zh'=2,'co'=2] {'zh','zl','x','co'}, dimensions={0} | all-to-all | bytes 262144 | tf_op jit(solution)/shard_map/all_to_all | solution.py:244
  123.0 0.9 shard_map.108
  123.8 15.4 %all_to_all.51.a = f32[32,24,128]{2,1,0:T(8,128)S(1)} all-to-all(f32[32,24,128]{2,1,0:T(8,128)S(1)} %bitcast.3), channel_id=1, replica_groups=mesh['x'=4,'zl'=8,'y'=4,'zh'=2,'co'=2] {'x','y','co'}, dimensions={0} | all-to-all | bytes 786432 | tf_op jit(solution)/shard_map/all_to_all | solution.py:244
  139.3 15.8 %all_to_all.52.a = f32[16,24,128]{2,1,0:T(8,128)S(1)} all-to-all(f32[16,24,128]{2,1,0:T(8,128)S(1)} %shard_map.109), channel_id=1, replica_groups=mesh['x'=4,'zl'=8,'y'=4,'zh'=2,'co'=2] {'zh','zl'}, dimensions={0} | all-to-all | bytes 393216 | tf_op jit(solution)/shard_map/all_to_all | solution.py:244
  155.1 17.1 %all_to_all.53 = f32[32,24,128]{2,1,0:T(8,128)S(1)} all-to-all(f32[32,24,128]{2,1,0:T(8,128)S(1)} %shard_map.110), channel_id=1, replica_groups=mesh['x'=4,'zl'=8,'y'=4,'zh'=2,'co'=2] {'x','y','co'}, dimensions={0} | all-to-all | bytes 786432 | tf_op jit(solution)/shard_map/all_to_all | solution.py:244
  172.2 1.3 shard_map.111
  (3 shorter events, 0.1 us)
Async XLA Ops:
  0.6 0.8 copy-start.2
  0.6 1.0 copy-start
  0.7 1.0 copy-start.1
  0.7 1.0 copy-start.5
  55.8 14.5 %copy-start.3 = (f32[8,16,128]{2,1,0:T(8,128)S(1)}, f32[8,16,128]{2,1,0:T(8,128)}, u32[]{:S(2)}) copy-start(f32[8,16,128]{2,1,0:T(8,128)} %cot_ref.3) | copy-start | bytes 196612
  55.8 14.4 %copy-start.4 = (f32[128,128]{1,0:T(8,128)S(1)}, f32[128,128]{1,0:T(8,128)}, u32[]{:S(2)}) copy-start(f32[128,128]{1,0:T(8,128)} %wout_ref.3) | copy-start | bytes 196612

commit v10 on v9

--- a/solution.py
+++ b/solution.py
@@ -67,7 +67,7 @@
         value = proj[128:256]
         sig = jax.nn.sigmoid(proj[0:128])
         masked = maskf * sig
-        msg_ref[:, 0, side * 128 : (side + 1) * 128] = masked * value
+        msg_ref[:, side, :] = masked * value
         factor_ref[base : base + 128] = masked
         factor_ref[base + 128 : base + 256] = value * (1.0 - sig)
     gate_ref[...] = jax.nn.sigmoid(dot(normed, wgate_ref[...], 1, 0))
@@ -84,12 +84,10 @@
     return [(x, co, zh) for x in range(4) for co in range(2) for zh in range(2)]
 
 
-def triangle_kernel(msg_ref, part_ref, left_ref, right_ref, flat_ref, rows_ref, turn_ref, natural_ref):
-    flat_ref[0, 0:128] = msg_ref[:, 0, 0:128]
-    flat_ref[1, 0:128] = msg_ref[:, 0, 128:256]
+def triangle_kernel(msg_ref, part_ref, left_ref, right_ref, rows_ref, turn_ref, natural_ref):
     for x, co, zh in channel_blocks():
         source, lanes = pl.ds(zh * 64 + x * 2 + co, 8, stride=8), slice(zh * 32 + co * 16, zh * 32 + co * 16 + 16)
-        left, right = flat_ref[0, source, :], flat_ref[1, source, :]
+        left, right = msg_ref[source, 0, :], msg_ref[source, 1, :]
         for s in range(8):
             rows_ref[x * 64 + s * 8 : x * 64 + s * 8 + 8, lanes] = left[:, s * 16 : (s + 1) * 16]
             turn_ref[s * 32 + x * 8 : s * 32 + x * 8 + 8, lanes] = right[:, s * 16 : (s + 1) * 16]
@@ -163,7 +161,7 @@
                 out_ref[(x * 4 + y) * 2 + co] = block
 
 
-def back_kernel(dtri_ref, left_ref, right_ref, msg_ref, flat_ref, rows_ref, natural_ref, turn_ref):
+def back_kernel(dtri_ref, left_ref, right_ref, msg_ref, rows_ref, natural_ref, turn_ref):
     right = right_ref[...]
     total = jnp.zeros((128, 128), F32)
     for x in range(4):
@@ -182,8 +180,7 @@
             turn_ref[1, co, zh, x, :, to] = d_right[x * 8 : (x + 1) * 8, lanes]
     for side in range(2):
         for x, co, zh in channel_blocks():
-            flat_ref[side, pl.ds(zh * 64 + x * 2 + co, 8, stride=8), :] = turn_ref[side, co, zh, x]
-        msg_ref[:, 0, side * 128 : (side + 1) * 128] = flat_ref[side, 0:128]
+            msg_ref[pl.ds(zh * 64 + x * 2 + co, 8, stride=8), side, :] = turn_ref[side, co, zh, x]
 
 
 def weights_kernel(
@@ -201,7 +198,7 @@
     weights_ref[640:768] = dot(normed_tri, cot * gate, 1, 0)
     for side in range(2):
         base = side * 256
-        d_value = msg_ref[:, 0, side * 128 : (side + 1) * 128] * factor_ref[base : base + 128]
+        d_value = msg_ref[:, side, :] * factor_ref[base : base + 128]
         d_gate = d_value * factor_ref[base + 128 : base + 256]
         dproj_ref[base : base + 128] = d_gate
         dproj_ref[base + 128 : base + 256] = d_value
@@ -252,7 +249,7 @@
         cost_estimate=pl.CostEstimate(flops=10**10, bytes_accessed=2**25, transcendentals=0),
         compiler_params=pltpu.CompilerParams(vmem_limit_bytes=4 * 1024 * 1024),
     )()
-    held = [(128, 1, 256), (512, 128), (128, 128), (128, 128)]
+    held = [(128, 2, 128), (512, 128), (128, 128), (128, 128)]
     return call(enter_kernel, held, [(8, 128)])(lanes, pair, pair_mask, w_in, w_gate)
 
 
@@ -274,7 +271,7 @@
     part, left, right = call(
         triangle_kernel,
         [(32, 16, 128), (512, 128), (128, 128)],
-        [(2, 144, 128), (256, 64), (256, 64), (264, 64)],
+        [(256, 64), (256, 64), (264, 64)],
     )(msg)
     part = swap(part, PLANE)
     (msg,) = call(home_kernel, [(16, 8, 128)], [(136, 128)])(part)
@@ -287,8 +284,8 @@
     d_tri = swap(d_tri, PLANE)
     (msg,) = call(
         back_kernel,
-        [(128, 1, 256)],
-        [(2, 144, 128), (256, 64), (264, 64), (2, 2, 2, 4, 8, 128)],
+        [(128, 2, 128)],
+        [(256, 64), (264, 64), (2, 2, 2, 4, 8, 128)],
     )(d_tri, left, right)
     msg = swap(msg, CHANNELS)
     weights, d_proj, d_pre, out_proj = call(

time: 174 us -> 174 us (level)
  no operation moved by 1% of the time
where the time goes in v10:
time: 174 us; the launch traced here: 173 us
  blocking collectives  166 us (95%)
  Pallas kernels  5.43 us (3%)
    all_to_all x9, blocking collectives, swap(): return lax.all_to_all(values, axes, split_axis=0, concat_axis=0, tiled=True)  166 us
    pallas_call x9, Pallas kernels, run(): pl.pallas_call(body, out_shape=[jax.ShapeDtypeStruct(s, F32) for s in out...  4.13 us

profile of v10, /device:TPU:1, one launch (start us, length us, event | category | flops | bytes accessed | tf_op | source)
XLA Modules:
  0.0 173.4 jit_solution(5494525519804926567)
XLA Ops:
  0.6 0.0 copy-start.2
  0.6 0.0 copy-start
  0.7 0.0 copy-start.1
  0.7 0.0 copy-start.5
  0.7 0.8 copy-done.2
  1.5 0.1 copy-done
  1.6 0.0 copy-done.1
  1.6 0.0 copy-done.5
  1.6 0.6 shard_map.102
  2.3 36.6 %all_to_all.45.msg_ref = f32[128,2,128]{2,1,0:T(2,128)S(1)} all-to-all(f32[128,2,128]{2,1,0:T(2,128)S(1)} %get-tuple-element.23), channel_id=1, replica_groups=mesh['x'=4,'zl'=8,'y'=4,'zh'=2,'co'=2] {'zh','zl','x','co'}, dimensions={0} | all-to-all | bytes 262144 | tf_op jit(solution)/shard_map/all_to_all | solution.py:241
  38.9 0.8 shard_map.103
  39.6 16.0 %all_to_all.46.part_ref = f32[32,16,128]{2,1,0:T(8,128)S(1)} all-to-all(f32[32,16,128]{2,1,0:T(8,128)S(1)} %get-tuple-element.24), channel_id=1, replica_groups=mesh['x'=4,'zl'=8,'y'=4,'zh'=2,'co'=2] {'x','y','co'}, dimensions={0} | all-to-all | bytes 524288 | tf_op jit(solution)/shard_map/all_to_all | solution.py:241
  55.6 0.1 shard_map.104
  55.8 0.0 copy-start.3
  55.8 0.0 copy-start.4
  55.8 14.4 %all_to_all.47.home_ref = f32[16,8,128]{2,1,0:T(8,128)S(1)} all-to-all(f32[16,8,128]{2,1,0:T(8,128)S(1)} %shard_map.104), channel_id=1, replica_groups=mesh['x'=4,'zl'=8,'y'=4,'zh'=2,'co'=2] {'zh','zl'}, dimensions={0} | all-to-all | bytes 131072 | tf_op jit(solution)/shard_map/all_to_all | solution.py:241
  70.2 0.0 copy-done.3
  70.2 0.0 copy-done.4
  70.2 0.5 shard_map.105
  70.8 15.1 %all_to_all.48.msg_ref = f32[16,8,128]{2,1,0:T(8,128)S(1)} all-to-all(f32[16,8,128]{2,1,0:T(8,128)S(1)} %get-tuple-element.26), channel_id=1, replica_groups=mesh['x'=4,'zl'=8,'y'=4,'zh'=2,'co'=2] {'zh','zl'}, dimensions={0} | all-to-all | bytes 131072 | tf_op jit(solution)/shard_map/all_to_all | solution.py:241
  85.8 0.1 shard_map.106
  86.0 14.4 %all_to_all.49.dtri_ref = f32[32,16,128]{2,1,0:T(8,128)S(1)} all-to-all(f32[32,16,128]{2,1,0:T(8,128)S(1)} %shard_map.106), channel_id=1, replica_groups=mesh['x'=4,'zl'=8,'y'=4,'zh'=2,'co'=2] {'x','y','co'}, dimensions={0} | all-to-all | bytes 524288 | tf_op jit(solution)/shard_map/all_to_all | solution.py:241
  100.4 1.0 shard_map.107
  101.4 21.4 %all_to_all.50.msg_ref = f32[128,2,128]{2,1,0:T(2,128)S(1)} all-to-all(f32[128,2,128]{2,1,0:T(2,128)S(1)} %shard_map.107), channel_id=1, replica_groups=mesh['x'=4,'zl'=8,'y'=4,'zh'=2,'co'=2] {'zh','zl','x','co'}, dimensions={0} | all-to-all | bytes 262144 | tf_op jit(solution)/shard_map/all_to_all | solution.py:241
  122.9 0.9 shard_map.108
  123.7 15.4 %all_to_all.51.a = f32[32,24,128]{2,1,0:T(8,128)S(1)} all-to-all(f32[32,24,128]{2,1,0:T(8,128)S(1)} %bitcast.3), channel_id=1, replica_groups=mesh['x'=4,'zl'=8,'y'=4,'zh'=2,'co'=2] {'x','y','co'}, dimensions={0} | all-to-all | bytes 786432 | tf_op jit(solution)/shard_map/all_to_all | solution.py:241
  139.2 15.8 %all_to_all.52.a = f32[16,24,128]{2,1,0:T(8,128)S(1)} all-to-all(f32[16,24,128]{2,1,0:T(8,128)S(1)} %shard_map.109), channel_id=1, replica_groups=mesh['x'=4,'zl'=8,'y'=4,'zh'=2,'co'=2] {'zh','zl'}, dimensions={0} | all-to-all | bytes 393216 | tf_op jit(solution)/shard_map/all_to_all | solution.py:241
  155.0 17.1 %all_to_all.53 = f32[32,24,128]{2,1,0:T(8,128)S(1)} all-to-all(f32[32,24,128]{2,1,0:T(8,128)S(1)} %shard_map.110), channel_id=1, replica_groups=mesh['x'=4,'zl'=8,'y'=4,'zh'=2,'co'=2] {'x','y','co'}, dimensions={0} | all-to-all | bytes 786432 | tf_op jit(solution)/shard_map/all_to_all | solution.py:241
  172.1 1.3 shard_map.111
  (3 shorter events, 0.1 us)
Async XLA Ops:
  0.6 0.8 copy-start.2
  0.6 1.0 copy-start
  0.7 1.0 copy-start.1
  0.7 1.0 copy-start.5
  55.8 14.5 %copy-start.3 = (f32[8,16,128]{2,1,0:T(8,128)S(1)}, f32[8,16,128]{2,1,0:T(8,128)}, u32[]{:S(2)}) copy-start(f32[8,16,128]{2,1,0:T(8,128)} %cot_ref.3) | copy-start | bytes 196612
  55.8 14.4 %copy-start.4 = (f32[128,128]{1,0:T(8,128)S(1)}, f32[128,128]{1,0:T(8,128)}, u32[]{:S(2)}) copy-start(f32[128,128]{1,0:T(8,128)} %wout_ref.3) | copy-start | bytes 196612

commit v11 on v9

--- a/solution.py
+++ b/solution.py
@@ -10,6 +10,7 @@
 CHANNELS = ("zh", "zl", "x", "co")
 PLANE = ("x", "y", "co")
 DEPTH = ("zh", "zl")
+SHARES = ("x", "co", "y")
 F32 = jnp.float32
 EPS = 1e-05
 
@@ -294,12 +295,12 @@
     weights, d_proj, d_pre, out_proj = call(
         weights_kernel, [(768, 128), (512, 128), (128, 128), (128, 128)]
     )(msg, factor, normed, tri, cotangent, gate, w_out)
-    parts = swap(weights.reshape(32, 24, 128), PLANE)
+    parts = swap(weights.reshape(32, 24, 128), SHARES)
     (parts,) = call(lambda a, b: sum_kernel(1.0, a, b), [(16, 24, 128)])(parts)
     parts = swap(parts, DEPTH)
     scale = 1.0 / (pair.shape[0] * lax.axis_size(ROW))
     (parts,) = call(lambda a, b: sum_kernel(scale, a, b), [(32, 24, 128)])(parts)
-    parts = swap(parts, PLANE)
+    parts = swap(parts, SHARES)
     d_pair, update, d_win, d_wgate, d_wout = leave(
         parts.reshape(768, 128), d_proj, d_pre, out_proj, gate, pair, w_in, w_gate
     )

time: 174 us -> 174 us (level)
  no operation moved by 1% of the time
where the time goes in v11:
time: 174 us; the launch traced here: 173 us
  blocking collectives  166 us (95%)
  Pallas kernels  5.53 us (3%)
    all_to_all x9, blocking collectives, swap(): return lax.all_to_all(values, axes, split_axis=0, concat_axis=0, tiled=True)  166 us
    pallas_call x9, Pallas kernels, run(): pl.pallas_call(body, out_shape=[jax.ShapeDtypeStruct(s, F32) for s in out...  4.23 us

profile of v11, /device:TPU:1, one launch (start us, length us, event | category | flops | bytes accessed | tf_op | source)
XLA Modules:
  0.0 173.5 jit_solution(3404165726097176684)
XLA Ops:
  0.6 0.0 copy-start.2
  0.6 0.0 copy-start
  0.7 0.0 copy-start.1
  0.7 0.0 copy-start.5
  0.7 0.8 copy-done.2
  1.5 0.1 copy-done
  1.6 0.0 copy-done.1
  1.6 0.0 copy-done.5
  1.6 0.6 shard_map.102
  2.3 36.6 %all_to_all.45.msg_ref = f32[128,1,256]{2,1,0:T(1,128)S(1)} all-to-all(f32[128,1,256]{2,1,0:T(1,128)S(1)} %get-tuple-element.23), channel_id=1, replica_groups=mesh['x'=4,'zl'=8,'y'=4,'zh'=2,'co'=2] {'zh','zl','x','co'}, dimensions={0} | all-to-all | bytes 262144 | tf_op jit(solution)/shard_map/all_to_all | solution.py:245
  38.9 0.8 shard_map.103
  39.7 16.0 %all_to_all.46.part_ref = f32[32,16,128]{2,1,0:T(8,128)S(1)} all-to-all(f32[32,16,128]{2,1,0:T(8,128)S(1)} %get-tuple-element.24), channel_id=1, replica_groups=mesh['x'=4,'zl'=8,'y'=4,'zh'=2,'co'=2] {'x','y','co'}, dimensions={0} | all-to-all | bytes 524288 | tf_op jit(solution)/shard_map/all_to_all | solution.py:245
  55.7 0.1 shard_map.104
  55.8 0.0 copy-start.3
  55.8 0.0 copy-start.4
  55.8 14.4 %all_to_all.47.home_ref = f32[16,8,128]{2,1,0:T(8,128)S(1)} all-to-all(f32[16,8,128]{2,1,0:T(8,128)S(1)} %shard_map.104), channel_id=1, replica_groups=mesh['x'=4,'zl'=8,'y'=4,'zh'=2,'co'=2] {'zh','zl'}, dimensions={0} | all-to-all | bytes 131072 | tf_op jit(solution)/shard_map/all_to_all | solution.py:245
  70.2 0.0 copy-done.3
  70.2 0.0 copy-done.4
  70.2 0.5 shard_map.105
  70.8 15.1 %all_to_all.48.msg_ref = f32[16,8,128]{2,1,0:T(8,128)S(1)} all-to-all(f32[16,8,128]{2,1,0:T(8,128)S(1)} %get-tuple-element.26), channel_id=1, replica_groups=mesh['x'=4,'zl'=8,'y'=4,'zh'=2,'co'=2] {'zh','zl'}, dimensions={0} | all-to-all | bytes 131072 | tf_op jit(solution)/shard_map/all_to_all | solution.py:245
  85.9 0.1 shard_map.106
  86.0 14.4 %all_to_all.49.dtri_ref = f32[32,16,128]{2,1,0:T(8,128)S(1)} all-to-all(f32[32,16,128]{2,1,0:T(8,128)S(1)} %shard_map.106), channel_id=1, replica_groups=mesh['x'=4,'zl'=8,'y'=4,'zh'=2,'co'=2] {'x','y','co'}, dimensions={0} | all-to-all | bytes 524288 | tf_op jit(solution)/shard_map/all_to_all | solution.py:245
  100.4 1.1 shard_map.107
  101.5 21.4 %all_to_all.50.msg_ref = f32[128,1,256]{2,1,0:T(1,128)S(1)} all-to-all(f32[128,1,256]{2,1,0:T(1,128)S(1)} %shard_map.107), channel_id=1, replica_groups=mesh['x'=4,'zl'=8,'y'=4,'zh'=2,'co'=2] {'zh','zl','x','co'}, dimensions={0} | all-to-all | bytes 262144 | tf_op jit(solution)/shard_map/all_to_all | solution.py:245
  123.0 0.9 shard_map.108
  123.8 15.1 %all_to_all.51.a = f32[32,24,128]{2,1,0:T(8,128)S(1)} all-to-all(f32[32,24,128]{2,1,0:T(8,128)S(1)} %bitcast.3), channel_id=1, replica_groups=mesh['x'=4,'zl'=8,'y'=4,'zh'=2,'co'=2] {'x','co','y'}, dimensions={0} | all-to-all | bytes 786432 | tf_op jit(solution)/shard_map/all_to_all | solution.py:245
  139.0 15.1 %all_to_all.52.a = f32[16,24,128]{2,1,0:T(8,128)S(1)} all-to-all(f32[16,24,128]{2,1,0:T(8,128)S(1)} %shard_map.109), channel_id=1, replica_groups=mesh['x'=4,'zl'=8,'y'=4,'zh'=2,'co'=2] {'zh','zl'}, dimensions={0} | all-to-all | bytes 393216 | tf_op jit(solution)/shard_map/all_to_all | solution.py:245
  154.2 18.0 %all_to_all.53 = f32[32,24,128]{2,1,0:T(8,128)S(1)} all-to-all(f32[32,24,128]{2,1,0:T(8,128)S(1)} %shard_map.110), channel_id=1, replica_groups=mesh['x'=4,'zl'=8,'y'=4,'zh'=2,'co'=2] {'x','co','y'}, dimensions={0} | all-to-all | bytes 786432 | tf_op jit(solution)/shard_map/all_to_all | solution.py:245
  172.2 1.3 shard_map.111
  (3 shorter events, 0.1 us)
Async XLA Ops:
  0.6 0.8 copy-start.2
  0.6 1.0 copy-start
  0.7 1.0 copy-start.1
  0.7 1.0 copy-start.5
  55.8 14.5 %copy-start.3 = (f32[8,16,128]{2,1,0:T(8,128)S(1)}, f32[8,16,128]{2,1,0:T(8,128)}, u32[]{:S(2)}) copy-start(f32[8,16,128]{2,1,0:T(8,128)} %cot_ref.3) | copy-start | bytes 196612
  55.8 14.4 %copy-start.4 = (f32[128,128]{1,0:T(8,128)S(1)}, f32[128,128]{1,0:T(8,128)}, u32[]{:S(2)}) copy-start(f32[128,128]{1,0:T(8,128)} %wout_ref.3) | copy-start | bytes 196612
